TPU v7x, 32 devices: a whole 2x2x4 slice. The times are simulated.
32 devices in a mesh: grp: 2 (over core), dp: 16 (over z, y, x).
Axes of the slice: x: 2, y: 2, z: 4, core: 2. Of those that a mesh axis runs over, the one named last changes fastest.
Arguments:
- tokens: bfloat16 [4096, 2048], P(('grp', 'dp')), may hold values from -6 to 6
- segments: int32 [4096], P('grp'), may hold values from 0 to 66, as said below
- routes: int32 [4096, 8], P(('grp', 'dp')), may hold values from 0 to 15, all different within a row; in each aligned block of 128 rows (0 to 127, 128 to 255, ...) at most 80 rows name the same one
- route_weight: float32 [4096, 8], P(('grp', 'dp')), may hold values from 0.06 to 0.19
- capacity: int32 [1], replicated, may hold values from 768 to 1279
- norm_gain: float32 [2, 2048], replicated, may hold values from 0.5 to 1.5
- qkv_weight: bfloat16 [6144, 2048], P('dp'), may hold values from -0.125 to 0.125
- out_weight: bfloat16 [2048, 2048], P('dp'), may hold values from -1 to 1
- gate_weight: bfloat16 [16, 2048, 1024], P('dp'), may hold values from -0.125 to 0.125
- up_weight: bfloat16 [16, 2048, 1024], P('dp'), may hold values from -0.125 to 0.125
- down_weight: bfloat16 [16, 1024, 2048], P('dp'), may hold values from -0.75 to 0.75
- cotangent: bfloat16 [4096, 2048], P(('grp', 'dp')), may hold values from -6 to 6
Outputs:
- layer_out: bfloat16 [4096, 2048], P(('grp', 'dp'))
- tokens_grad: float32 [4096, 2048], P(('grp', 'dp'))
- qkv_weight_grad: float32 [6144, 2048], P('dp')
- out_weight_grad: float32 [2048, 2048], P('dp')
- gate_weight_grad: float32 [16, 2048, 1024], P('dp')
- up_weight_grad: float32 [16, 2048, 1024], P('dp')
- down_weight_grad: float32 [16, 1024, 2048], P('dp')
- norm_gain_grad: float32 [2, 2048], replicated
- stats: float32 [2, 3], P('grp')
Inputs may be any that keep to these rules, and one draw needn't show every extreme that they name: `segments`: in each sequence of 2048 tokens, numbers never fall except to 0, which marks the padding that ends the sequence; one document covers all but at most 64 tokens at each end. `routes`: A token names 8 different experts; among the 128 tokens of one device no expert is named more than 80 times.
All inputs are finite; a program needn't handle non-finite values.
Results may differ from a plain program's by a relative error of at most 0.023.
Values may be sent and summed in bfloat16 or wider, within the bound.
A program may use at most 384 MiB of HBM per device.

v0:
```python
import jax
import jax.numpy as jnp
from jax import lax
from jax.sharding import PartitionSpec as P

H = 16
HD = 128
TOPK = 8


EPS = 1e-06
THETA = 50000.0


def prefix(shard, axis, combine, identity):
    length, place = (lax.axis_size(axis), lax.axis_index(axis))
    everything = lax.all_gather(shard, axis)
    start = jnp.broadcast_to(jnp.asarray(identity, shard.dtype), shard.shape)

    def step(k, before):
        reached = k < place
        new = combine(before, everything[k])
        return jnp.where(reached, new, before)

    return lax.fori_loop(0, length, step, start)


def rmsnorm(field, gain_row):
    return field * lax.rsqrt(jnp.mean(field * field, -1, keepdims=True) + EPS) * gain_row


def rotary_tables(length, offset):
    position = (offset + jnp.arange(length)).astype(jnp.float32)
    freq = THETA ** (-(jnp.arange(HD // 2).astype(jnp.float32) * 2.0 / HD))
    angle = position[:, None] * freq[None, :]
    return (jnp.cos(angle)[:, None, :], jnp.sin(angle)[:, None, :])


def rotate(heads_in, cos_table, sin_table):
    half_size = heads_in.shape[-1] // 2
    first = heads_in[..., :half_size]
    second = heads_in[..., half_size:]
    return jnp.concatenate(
        [first * cos_table - second * sin_table, second * cos_table + first * sin_table], -1
    )


def add_counts(earlier, later):
    return earlier + later


def regroup(buffer_in, devices, local_experts, slot_most):
    model_width = buffer_in.shape[-1]
    shaped = buffer_in.reshape(devices, local_experts, slot_most, model_width)
    return shaped.transpose(1, 0, 2, 3).reshape(local_experts, devices * slot_most, model_width)


def ungroup(buffer_in, devices, local_experts, slot_most):
    model_width = buffer_in.shape[-1]
    shaped = buffer_in.reshape(local_experts, devices, slot_most, model_width)
    return shaped.transpose(1, 0, 2, 3).reshape(devices, local_experts * slot_most, model_width)


def score_heads(queries, keys_all):
    scale_factor = HD ** (-0.5)
    return (
        jnp.einsum("qhd,khd->hqk", queries, keys_all, preferred_element_type=jnp.float32)
        * scale_factor
    )


def attention_probs(queries, keys_all, allowed):
    scores = score_heads(queries, keys_all)
    masked = jnp.where(allowed[None], scores, -1e30)
    peak = jnp.max(masked, -1, keepdims=True)
    expo = jnp.where(allowed[None], jnp.exp(masked - peak), 0.0)
    row_total = jnp.sum(expo, -1, keepdims=True)
    return (expo / jnp.maximum(row_total, 1.0), peak, row_total)


def probs_from(scores, allowed, peak, row_total):
    masked = jnp.where(allowed[None], scores, -1e30)
    expo = jnp.where(allowed[None], jnp.exp(masked - peak), 0.0)
    return expo / jnp.maximum(row_total, 1.0)


def per_device(
    tokens,
    segments,
    routes,
    route_weight,
    capacity,
    norm_gain,
    qkv_weight,
    out_weight,
    gate_weight,
    up_weight,
    down_weight,
    cotangent,
):
    tok_count = tokens.shape[0]
    model_width = tokens.shape[1]
    devices = lax.axis_size("dp")
    my_index = lax.axis_index("dp")
    local_experts = gate_weight.shape[0]
    experts = devices * local_experts
    slot_most = min(tok_count, tok_count * TOPK * 5 // (4 * experts))
    seq_len = segments.shape[0]
    pair_count = tok_count * TOPK
    scale_factor = HD ** (-0.5)
    own_seg = lax.dynamic_slice_in_dim(segments, my_index * tok_count, tok_count)
    allowed = (own_seg[:, None] == segments[None, :]) & (segments[None, :] != 0)
    cos_table, sin_table = rotary_tables(tok_count, my_index * tok_count)
    stream = tokens.astype(jnp.float32)
    normed_low = rmsnorm(stream, norm_gain[0]).astype(jnp.bfloat16)
    dense_qkv, dense_out = (
        lax.all_gather(qkv_weight, "dp", axis=0, tiled=True),
        lax.all_gather(out_weight, "dp", axis=0, tiled=True),
    )
    projected = lax.dot_general(
        normed_low, dense_qkv, (((1,), (1,)), ((), ())), preferred_element_type=jnp.float32
    )
    queries = rotate(
        projected[:, :model_width].reshape(tok_count, H, HD), cos_table, sin_table
    ).astype(jnp.bfloat16)
    keys_own = rotate(
        projected[:, model_width : 2 * model_width].reshape(tok_count, H, HD), cos_table, sin_table
    )
    keys_own = keys_own.reshape(tok_count, model_width).astype(jnp.bfloat16)
    values_own = projected[:, 2 * model_width :].astype(jnp.bfloat16)
    keys_all, values_all = (
        lax.all_gather(keys_own, "dp", axis=0, tiled=True),
        lax.all_gather(values_own, "dp", axis=0, tiled=True),
    )
    keys_heads = keys_all.reshape(seq_len, H, HD)
    values_heads = values_all.reshape(seq_len, H, HD)
    attn_prob, peak, row_total = attention_probs(queries, keys_heads, allowed)
    prob_low = attn_prob.astype(jnp.bfloat16)
    context = jnp.einsum("hqk,khd->qhd", prob_low, values_heads, preferred_element_type=jnp.float32)
    context = context.reshape(tok_count, model_width).astype(jnp.bfloat16)
    attended = lax.dot_general(
        context, dense_out, (((1,), (1,)), ((), ())), preferred_element_type=jnp.float32
    )
    middle = stream + attended
    normed2_low = rmsnorm(middle, norm_gain[1]).astype(jnp.bfloat16)
    flat_routes = routes.reshape(-1)
    one_hot = (flat_routes[:, None] == jnp.arange(experts, dtype=jnp.int32)[None, :]).astype(
        jnp.int32
    )
    before = prefix(
        jnp.sum(one_hot, 0, dtype=jnp.int32), "dp", add_counts, jnp.zeros((experts,), jnp.int32)
    )
    running = jnp.cumsum(one_hot, 0, dtype=jnp.int32) - one_hot
    local_rank = jnp.sum(running * one_hot, 1, dtype=jnp.int32)
    group_rank = local_rank + jnp.sum(one_hot * before[None, :], 1, dtype=jnp.int32)
    keep_mask = group_rank < capacity[0]
    slot_index = flat_routes * slot_most + local_rank
    target = jnp.where(keep_mask, slot_index, experts * slot_most)
    slot_table = (
        jnp.full((experts * slot_most,), pair_count, jnp.int32)
        .at[target]
        .set(jnp.arange(pair_count, dtype=jnp.int32), mode="drop")
    )
    live_slot = slot_table < pair_count
    pair_of = jnp.minimum(slot_table, pair_count - 1)
    token_of = pair_of // TOPK
    outbox = jnp.where(live_slot[:, None], normed2_low[token_of], jnp.zeros((), jnp.bfloat16))
    outbox = outbox.reshape(devices, local_experts * slot_most, model_width)
    arrived = lax.all_to_all(outbox, "dp", split_axis=0, concat_axis=0, tiled=True)
    expert_rows = regroup(arrived, devices, local_experts, slot_most)
    gate_act = jnp.einsum(
        "erd,edf->erf", expert_rows, gate_weight, preferred_element_type=jnp.float32
    )
    up_act = jnp.einsum("erd,edf->erf", expert_rows, up_weight, preferred_element_type=jnp.float32)
    sigmoid_gate = jax.nn.sigmoid(gate_act)
    hidden = (gate_act * sigmoid_gate * up_act).astype(jnp.bfloat16)
    expert_out = jnp.einsum(
        "erf,efd->erd", hidden, down_weight, preferred_element_type=jnp.float32
    ).astype(jnp.bfloat16)
    returned = lax.all_to_all(
        ungroup(expert_out, devices, local_experts, slot_most),
        "dp",
        split_axis=0,
        concat_axis=0,
        tiled=True,
    )
    returned = returned.reshape(experts * slot_most, model_width)
    safe_slot = jnp.where(keep_mask, slot_index, 0)
    route_coef = jnp.where(keep_mask, route_weight.reshape(-1), 0.0)
    picked = returned[safe_slot].astype(jnp.float32)
    mixture = jnp.sum((route_coef[:, None] * picked).reshape(tok_count, TOPK, model_width), 1)
    layer_sum = middle + mixture
    valid_rows = (own_seg != 0).astype(jnp.float32)
    stat_sums = jnp.stack(
        [
            jnp.sum(valid_rows * jnp.sum(layer_sum * layer_sum, -1)),
            jnp.sum(valid_rows * jnp.sum(attended * attended, -1)),
            jnp.sum(valid_rows * jnp.sum(mixture * mixture, -1)),
            jnp.sum(valid_rows) * model_width,
        ]
    )
    grad_out = cotangent.astype(jnp.float32)
    pair_grad = (
        (route_coef.reshape(tok_count, TOPK, 1) * grad_out[:, None, :])
        .reshape(pair_count, model_width)
        .astype(jnp.bfloat16)
    )
    grad_box = jnp.where(live_slot[:, None], pair_grad[pair_of], jnp.zeros((), jnp.bfloat16))
    grad_box = grad_box.reshape(devices, local_experts * slot_most, model_width)
    out_grad_rows = regroup(
        lax.all_to_all(grad_box, "dp", split_axis=0, concat_axis=0, tiled=True),
        devices,
        local_experts,
        slot_most,
    )
    hidden_grad = jnp.einsum(
        "erd,efd->erf", out_grad_rows, down_weight, preferred_element_type=jnp.float32
    )
    gate_grad = (
        hidden_grad * up_act * sigmoid_gate * (1.0 + gate_act * (1.0 - sigmoid_gate))
    ).astype(jnp.bfloat16)
    up_grad = (hidden_grad * gate_act * sigmoid_gate).astype(jnp.bfloat16)
    down_part = jnp.einsum(
        "erf,erd->efd", hidden, out_grad_rows, preferred_element_type=jnp.float32
    )
    gate_part = jnp.einsum(
        "erd,erf->edf", expert_rows, gate_grad, preferred_element_type=jnp.float32
    )
    up_part = jnp.einsum("erd,erf->edf", expert_rows, up_grad, preferred_element_type=jnp.float32)
    row_grad = jnp.einsum(
        "erf,edf->erd", gate_grad, gate_weight, preferred_element_type=jnp.float32
    )
    row_grad = (
        row_grad
        + jnp.einsum("erf,edf->erd", up_grad, up_weight, preferred_element_type=jnp.float32)
    ).astype(jnp.bfloat16)
    back_rows = lax.all_to_all(
        ungroup(row_grad, devices, local_experts, slot_most),
        "dp",
        split_axis=0,
        concat_axis=0,
        tiled=True,
    )
    back_rows = back_rows.reshape(experts * slot_most, model_width)
    pair_back = jnp.where(keep_mask[:, None], back_rows[safe_slot].astype(jnp.float32), 0.0)
    normed2_grad = jnp.sum(pair_back.reshape(tok_count, TOPK, model_width), 1)
    norm2_pull = jax.vjp(rmsnorm, middle, norm_gain[1])[1]
    middle_norm_grad, gain2_grad = norm2_pull(normed2_grad)
    middle_grad = grad_out + middle_norm_grad
    attended_grad = middle_grad.astype(jnp.bfloat16)
    context_grad = jnp.dot(attended_grad, dense_out, preferred_element_type=jnp.float32).astype(
        jnp.bfloat16
    )
    context_heads = context_grad.reshape(tok_count, H, HD)
    prob_again = probs_from(score_heads(queries, keys_heads), allowed, peak, row_total)
    prob_grad = jnp.einsum(
        "qhd,khd->hqk", context_heads, values_heads, preferred_element_type=jnp.float32
    )
    row_delta = jnp.sum(prob_again * prob_grad, -1, keepdims=True)
    score_grad = (prob_again * (prob_grad - row_delta)).astype(jnp.bfloat16)
    query_grad = (
        jnp.einsum("hqk,khd->qhd", score_grad, keys_heads, preferred_element_type=jnp.float32)
        * scale_factor
    )
    queries_all, context_grad_all = (
        lax.all_gather(queries.reshape(tok_count, model_width), "dp", axis=0, tiled=True),
        lax.all_gather(context_grad, "dp", axis=0, tiled=True),
    )
    peak_all, total_all, delta_all = (
        lax.all_gather(peak[:, :, 0].T, "dp", axis=0, tiled=True),
        lax.all_gather(row_total[:, :, 0].T, "dp", axis=0, tiled=True),
        lax.all_gather(row_delta[:, :, 0].T, "dp", axis=0, tiled=True),
    )
    query_heads_all = queries_all.reshape(seq_len, H, HD)
    context_grad_heads = context_grad_all.reshape(seq_len, H, HD)
    key_allowed = (segments[:, None] == own_seg[None, :]) & (own_seg[None, :] != 0)
    keys_mine = keys_own.reshape(tok_count, H, HD)
    values_mine = values_own.reshape(tok_count, H, HD)
    prob_key = probs_from(
        score_heads(query_heads_all, keys_mine),
        key_allowed,
        peak_all.T[:, :, None],
        total_all.T[:, :, None],
    )
    prob_grad_key = jnp.einsum(
        "qhd,khd->hqk", context_grad_heads, values_mine, preferred_element_type=jnp.float32
    )
    score_grad_key = (prob_key * (prob_grad_key - delta_all.T[:, :, None])).astype(jnp.bfloat16)
    key_grad = (
        jnp.einsum(
            "hqk,qhd->khd", score_grad_key, query_heads_all, preferred_element_type=jnp.float32
        )
        * scale_factor
    )
    value_grad = jnp.einsum(
        "hqk,qhd->khd",
        prob_key.astype(jnp.bfloat16),
        context_grad_heads,
        preferred_element_type=jnp.float32,
    )
    value_grad = value_grad.reshape(tok_count, model_width)
    query_back = rotate(query_grad, cos_table, -sin_table).reshape(tok_count, model_width)
    key_back = rotate(key_grad, cos_table, -sin_table).reshape(tok_count, model_width)
    projected_grad = jnp.concatenate([query_back, key_back, value_grad], 1).astype(jnp.bfloat16)
    share_rows = model_width // devices
    qkv_rows = lax.dot_general(
        projected_grad, normed_low, (((0,), (0,)), ((), ())), preferred_element_type=jnp.float32
    )
    out_rows = lax.dot_general(
        attended_grad, context, (((0,), (0,)), ((), ())), preferred_element_type=jnp.float32
    )
    dense_part = lax.psum_scatter(
        jnp.concatenate(
            [qkv_rows.reshape(lax.axis_size("dp") * share_rows, 3 * model_width), out_rows], 1
        ).astype(jnp.bfloat16),
        "dp",
        scatter_dimension=0,
        tiled=True,
    ).astype(jnp.float32)
    qkv_grad_part = dense_part[:, : 3 * model_width].reshape(3 * share_rows, model_width)
    out_grad_part = dense_part[:, 3 * model_width :]
    normed_grad = jnp.dot(projected_grad, dense_qkv, preferred_element_type=jnp.float32)
    norm1_pull = jax.vjp(rmsnorm, stream, norm_gain[0])[1]
    stream_norm_grad, gain1_grad = norm1_pull(normed_grad)
    tokens_grad = middle_grad + stream_norm_grad
    seq_sums, gain_dp = lax.psum((stat_sums, jnp.stack([gain1_grad, gain2_grad])), "dp")
    stat_row = jnp.sqrt(seq_sums[:3] / seq_sums[3]).reshape(1, 3)
    qkv_total, out_total, gate_total, up_total, down_total, gain_total = (
        lax.psum(qkv_grad_part.astype(jnp.bfloat16), "grp").astype(jnp.float32),
        lax.psum(out_grad_part.astype(jnp.bfloat16), "grp").astype(jnp.float32),
        lax.psum(gate_part.astype(jnp.bfloat16), "grp").astype(jnp.float32),
        lax.psum(up_part.astype(jnp.bfloat16), "grp").astype(jnp.float32),
        lax.psum(down_part.astype(jnp.bfloat16), "grp").astype(jnp.float32),
        lax.psum(gain_dp.astype(jnp.bfloat16), "grp").astype(jnp.float32),
    )
    return (
        layer_sum.astype(jnp.bfloat16),
        tokens_grad,
        qkv_total,
        out_total,
        gate_total,
        up_total,
        down_total,
        gain_total,
        stat_row,
    )


def solution(mesh):
    in_specs = (
        P(("grp", "dp"), None),
        P("grp"),
        P(("grp", "dp"), None),
        P(("grp", "dp"), None),
        P(),
        P(),
        P("dp", None),
        P("dp", None),
        P("dp", None, None),
        P("dp", None, None),
        P("dp", None, None),
        P(("grp", "dp"), None),
    )
    out_specs = (
        P(("grp", "dp"), None),
        P(("grp", "dp"), None),
        P("dp", None),
        P("dp", None),
        P("dp", None, None),
        P("dp", None, None),
        P("dp", None, None),
        P(),
        P("grp", None),
    )
    return jax.shard_map(
        per_device, mesh=mesh, in_specs=in_specs, out_specs=out_specs, check_vma=False
    )
```

profile of v0, /device:TPU:5, one launch (start us, length us, event | category | flops | bytes accessed | tf_op | source)
XLA Modules:
  0.0 2439.3 jit_solution(12577087290788741543)
XLA Ops:
  11.5 271.4 %all-gather.8.cloned.1.call-done = bf16[6144,2048]{1,0:T(8,128)(2,1)} async-done(((bf16[384,2048]{1,0:T(8,128)(2,1)}), bf16[6144,2048]{1,0:T(8,128)(2,1)}) %all-gather.8.cloned.1.call-update) | async-done | bytes 25165840 | tf_op jit(solution)/shard_map/all_gather | solution.py:117
  282.8 13.4 fusion.57
  297.6 2.3 multiply_subtract_fusion
  301.0 2.0 copy.42
  307.3 8.5 all-reduce
  315.9 4.5 reduce-window.6
  322.2 4.5 scatter_custom_fusion
  329.5 2.5 fusion.11
  332.0 13.6 gather_fusion.2
  346.8 97.0 %all-gather.12.cloned.1.call-done = bf16[2048,2048]{0,1:T(8,128)(2,1)} async-done(((bf16[128,2048]{0,1:T(8,128)(2,1)}), bf16[2048,2048]{0,1:T(8,128)(2,1)}) %all-gather.12.cloned.1.call-update) | async-done | bytes 8388624 | tf_op jit(solution)/shard_map/all_gather | solution.py:132
  443.8 6.1 fusion
  449.9 5.0 fusion.2
  456.0 101.3 %all-gather.10.cloned.1.call-done = bf16[2048,2048]{1,0:T(8,128)(2,1)} async-done(((bf16[128,2048]{1,0:T(8,128)(2,1)}), bf16[2048,2048]{1,0:T(8,128)(2,1)}) %all-gather.10.cloned.1.call-update) | async-done | bytes 8388624 | tf_op jit(solution)/shard_map/all_gather | solution.py:133
  557.2 11.6 fusion.38
  568.9 102.0 %all-gather.14.cloned.1.call-done = bf16[2048,2048]{1,0:T(8,128)(2,1)} async-done(((bf16[128,2048]{1,0:T(8,128)(2,1)}), bf16[2048,2048]{1,0:T(8,128)(2,1)}) %all-gather.14.cloned.1.call-update) | async-done | bytes 8388624 | tf_op jit(solution)/shard_map/all_gather | solution.py:118
  670.9 6.9 multiply_reduce_fusion.6
  678.0 6.1 gather_fusion
  684.1 8.9 broadcast_select_fusion.2
  693.0 119.0 %all_to_all.20 = bf16[16,80,2048]{2,1,0:T(8,128)(2,1)} all-to-all(bf16[16,80,2048]{2,1,0:T(8,128)(2,1)} %get-tuple-element.167), channel_id=1, replica_groups=mesh['grp'=2,'dp'=16] {'dp'}, dimensions={0} | all-to-all | bytes 10485760 | tf_op jit(solution)/shard_map/all_to_all | solution.py:169
  812.0 6.0 all-to-all-start.2
  818.1 10.4 fusion.25
  828.4 7.3 fusion.29
  835.7 84.6 %all-to-all-done.2 = bf16[16,80,2048]{2,1,0:T(8,128)(2,1)} async-done(((bf16[16,80,2048]{2,1,0:T(8,128)(2,1)}), bf16[16,80,2048]{2,1,0:T(8,128)(2,1)}, u32[]{:S(2)}, u32[]{:S(2)}) %all-to-all-start.2) | async-done | bytes 5242912 | tf_op jit(solution)/shard_map/all_to_all | solution.py:211
  920.3 15.1 multiply_convert_fusion.4
  935.4 7.3 convolution_convert_fusion.1
  942.8 18.1 all-to-all-start.1
  962.0 8.7 fusion.27
  970.7 7.6 add_convert_fusion
  978.3 119.6 %all-to-all-done.1 = bf16[16,80,2048]{2,1,0:T(8,128)(2,1)} async-done(((bf16[16,80,2048]{2,1,0:T(8,128)(2,1)}), bf16[16,80,2048]{2,1,0:T(8,128)(2,1)}, u32[]{:S(2)}, u32[]{:S(2)}) %all-to-all-start.1) | async-done | bytes 5242912 | tf_op jit(solution)/shard_map/all_to_all | solution.py:180
  1097.9 47.7 %all-to-all-start.3 = ((bf16[16,80,2048]{2,1,0:T(8,128)(2,1)}), bf16[16,80,2048]{2,1,0:T(8,128)(2,1)}, u32[]{:S(2)}, u32[]{:S(2)}) async-start(bf16[16,80,2048]{2,1,0:T(8,128)(2,1)} %bitcast.177), calls=%async_computation.3 | async-start | bytes 10485760 | tf_op jit(solution)/shard_map/all_to_all | solution.py:237
  1145.7 12.0 gather_fusion.1
  1157.7 119.4 %all-to-all-done.3 = bf16[16,80,2048]{2,1,0:T(8,128)(2,1)} async-done(((bf16[16,80,2048]{2,1,0:T(8,128)(2,1)}), bf16[16,80,2048]{2,1,0:T(8,128)(2,1)}, u32[]{:S(2)}, u32[]{:S(2)}) %all-to-all-start.3) | async-done | bytes 5242912 | tf_op jit(solution)/shard_map/all_to_all | solution.py:237
  1277.1 12.2 gather_fusion.3
  1289.3 6.7 fusion.10
  1296.0 6.8 fusion.9
  1305.2 2.1 convolution_convert_fusion.3
  1308.8 41.1 %all_gather.41 = f32[2048,16]{0,1:T(8,128)S(1)} all-gather(f32[128,16]{0,1:T(8,128)S(1)} %bitcast.199), channel_id=1, replica_groups=mesh['grp'=2,'dp'=16] {'dp'}, dimensions={0}, use_global_device_ids=true | all-gather | bytes 139264 | tf_op jit(solution)/shard_map/all_gather | solution.py:271
  1349.9 30.8 %all_gather.40 = f32[2048,16]{0,1:T(8,128)S(1)} all-gather(f32[128,16]{0,1:T(8,128)S(1)} %bitcast.200), channel_id=1, replica_groups=mesh['grp'=2,'dp'=16] {'dp'}, dimensions={0}, use_global_device_ids=true | all-gather | bytes 139264 | tf_op jit(solution)/shard_map/all_gather | solution.py:270
  1380.7 14.8 select_divide_fusion
  1395.5 5.7 convolution_convert_fusion.2
  1401.3 12.3 copy.60
  1413.6 15.4 multiply_reduce_fusion
  1429.0 31.3 %all_gather.43 = f32[2048,16]{0,1:T(8,128)S(1)} all-gather(f32[128,16]{0,1:T(8,128)S(1)} %bitcast.207), channel_id=1, replica_groups=mesh['grp'=2,'dp'=16] {'dp'}, dimensions={0}, use_global_device_ids=true | all-gather | bytes 139264 | tf_op jit(solution)/shard_map/all_gather | solution.py:272
  1460.3 18.2 fusion.32
  1478.5 12.2 copy.72
  1490.7 10.6 fusion.35
  1501.3 15.7 fusion.34
  1521.4 17.9 convolution_convert_fusion
  1539.3 36.0 %reshape.544 = bf16[2048,6144]{1,0:T(8,128)(2,1)} reshape(bf16[6144,2048]{1,0:T(8,128)(2,1)} %convolution_convert_fusion) | data formatting | bytes 50331648 | tf_op jit(solution)/shard_map/reshape | solution.py:314
  1575.3 22.8 pad_maximum_fusion
  1598.2 10.5 convert_bitcast_fusion
  1608.7 9.9 convert_bitcast_fusion.1
  1618.6 7.2 convert_bitcast_fusion.2
  1625.8 678.3 %reduce-scatter.2.cloned.1.call-done = bf16[128,8192]{1,0:T(8,128)(2,1)} async-done(((bf16[2048,8192]{1,0:T(8,128)(2,1)}), bf16[128,8192]{1,0:T(8,128)(2,1)}) %reduce-scatter.2.cloned.1.call-update) | async-done | bytes 2097168 | tf_op jit(solution)/shard_map/reduce_scatter | solution.py:312
  2307.6 2.0 slice.103
  2312.9 12.7 fusion.46
  2325.7 64.8 %all-reduce.1 = (bf16[2,2048]{1,0:T(2,128)(2,1)S(1)}, f32[4]{0:T(128)S(1)}) all-reduce(f32[2,2048]{1,0:T(2,128)S(1)} %pad_maximum_fusion.6, f32[4]{0:T(128)S(1)} %pad_maximum_fusion.7), channel_id=1, replica_groups=mesh['grp'=2,'dp'=16] {'dp'}, use_global_device_ids=true, to_apply=%region_25.26 | all-reduce | flops 4100 | bytes 24608 | tf_op jit(solution)/shard_map/psum | solution.py:326
  2391.0 17.4 psum.62
  2410.2 2.5 fusion.48
  2412.7 2.3 convert_element_type.199
  2415.0 3.6 convert_element_type.198
  2418.6 4.4 convert_element_type.202
  2423.0 4.4 convert_element_type.205
  2427.5 4.4 convert_element_type.208
  (247 shorter events, 34.5 us)
Async XLA Ops:
  7.2 275.7 %all-gather.8.cloned.1.call-start = ((), (), s32[]{:S(2)}) async-start(), calls=%async_computation.5 | async-start | bytes 26738688 | tf_op jit(solution)/shard_map/all_gather | solution.py:117
  7.9 435.8 %all-gather.12.cloned.1.call-start = ((), (), s32[]{:S(2)}) async-start(), calls=%async_computation.7 | async-start | bytes 8912896 | tf_op jit(solution)/shard_map/all_gather | solution.py:132
  9.7 286.5 %copy-start.42 = (f32[128]{0:T(128)}, f32[128]{0:T(128)S(1)}, u32[]{:S(2)}) copy-start(f32[128]{0:T(128)S(1)} %fusion.67) | copy-start | bytes 1540
  10.7 286.9 %copy-start.26 = (f32[128,64]{1,0:T(8,128)}, f32[128,64]{1,0:T(8,128)S(1)}, u32[]{:S(2)}) copy-start(f32[128,64]{1,0:T(8,128)S(1)} %get-tuple-element.170) | copy-start | bytes 98308
  11.5 284.7 %copy-start.30 = (f32[1,2048]{1,0:T(1,128)}, f32[1,2048]{1,0:T(1,128)S(1)}, u32[]{:S(2)}) copy-start(f32[1,2048]{1,0:T(1,128)S(1)} %get-tuple-element.161) | copy-start | bytes 24580
  296.8 7.7 copy-start.40
  296.8 8.9 copy-start.59
  297.6 29.4 %copy-start.49 = (f32[128,8]{0,1:T(8,128)S(1)}, f32[128,8]{0,1:T(8,128)}, u32[]{:S(2)}) copy-start(f32[128,8]{0,1:T(8,128)} %param.17) | copy-start | bytes 12292
  303.1 254.2 %all-gather.10.cloned.1.call-start = ((), (), s32[]{:S(2)}) async-start(), calls=%async_computation.6 | async-start | bytes 8912896 | tf_op jit(solution)/shard_map/all_gather | solution.py:133
  304.0 366.9 %all-gather.14.cloned.1.call-start = ((), (), s32[]{:S(2)}) async-start(), calls=%async_computation.8 | async-start | bytes 8912896 | tf_op jit(solution)/shard_map/all_gather | solution.py:118
  332.0 13.6 copy-start.35
  332.0 14.5 copy-start.21
  332.0 14.5 copy-start.22
  346.2 103.7 %copy-start.44 = (s32[128]{0:T(128)}, s32[128]{0:T(128)S(1)}, u32[]{:S(2)}) copy-start(s32[128]{0:T(128)S(1)} %get-tuple-element.134) | copy-start | bytes 1540
  346.4 210.8 %copy-start.13 = (pred[128,2048]{1,0:T(8,128)(4,1)}, pred[128,2048]{1,0:T(8,128)(4,1)S(1)}, u32[]{:S(2)}) copy-start(pred[128,2048]{1,0:T(8,128)(4,1)S(1)} %compare_and_fusion.1) | copy-start | bytes 786436
  449.9 6.1 copy-start
  455.9 112.9 %copy-start.37 = (f32[16,128]{1,0:T(8,128)}, f32[16,128]{1,0:T(8,128)S(1)}, u32[]{:S(2)}) copy-start(f32[16,128]{1,0:T(8,128)S(1)} %fusion.2) | copy-start | bytes 24580
  456.0 112.9 %copy-start.47 = (f32[16,128]{1,0:T(8,128)}, f32[16,128]{1,0:T(8,128)S(1)}, u32[]{:S(2)}) copy-start(f32[16,128]{1,0:T(8,128)S(1)} %broadcast_maximum_fusion) | copy-start | bytes 24580
  456.0 214.9 %copy-start.3 = (bf16[128,2048]{1,0:T(8,128)(2,1)S(1)}, bf16[128,2048]{1,0:T(8,128)(2,1)}, u32[]{:S(2)}) copy-start(bf16[128,2048]{1,0:T(8,128)(2,1)} %param.14) | copy-start | bytes 1572868
  568.9 115.2 %copy-start.18 = (bf16[16,128,128]{2,1,0:T(8,128)(2,1)}, bf16[16,128,128]{2,1,0:T(8,128)(2,1)S(1)}, u32[]{:S(2)}) copy-start(bf16[16,128,128]{2,1,0:T(8,128)(2,1)S(1)} %fusion.38) | copy-start | bytes 1572868
  812.0 108.3 %all-to-all-start.2 = ((bf16[16,80,2048]{2,1,0:T(8,128)(2,1)}), bf16[16,80,2048]{2,1,0:T(8,128)(2,1)}, u32[]{:S(2)}, u32[]{:S(2)}) async-start(bf16[16,80,2048]{2,1,0:T(8,128)(2,1)} %get-tuple-element.166), calls=%async_computation.2 | async-start | bytes 10485760 | tf_op jit(solution)/shard_map/all_to_all | solution.py:211
  818.0 10.4 copy-start.5
  818.0 10.4 copy-start.57
  920.3 15.1 copy-start.56
  935.4 7.4 copy-start.60
  942.8 155.1 %all-to-all-start.1 = ((bf16[16,80,2048]{2,1,0:T(8,128)(2,1)}), bf16[16,80,2048]{2,1,0:T(8,128)(2,1)}, u32[]{:S(2)}, u32[]{:S(2)}) async-start(bf16[16,80,2048]{2,1,0:T(8,128)(2,1)} %bitcast.176), calls=%async_computation.1 | async-start | bytes 10485760 | tf_op jit(solution)/shard_map/all_to_all | solution.py:180
  960.9 419.8 %all-gather.16.cloned.1.call-start = ((), (), s32[]{:S(2)}) async-start(), calls=%async_computation.9 | async-start | bytes 8912896 | tf_op jit(solution)/shard_map/all_gather | solution.py:266
  962.0 8.7 copy-start.58
  962.0 8.7 copy-start.61
  978.3 167.4 %copy-start.41 = (s32[1024,1]{0,1:T(1,128)S(1)}, s32[1024,1]{0,1:T(1,128)}, u32[]{:S(2)}) copy-start(s32[1024,1]{0,1:T(1,128)} %get-tuple-element.162) | copy-start | bytes 12292
  1097.9 179.2 %all-to-all-start.3 = ((bf16[16,80,2048]{2,1,0:T(8,128)(2,1)}), bf16[16,80,2048]{2,1,0:T(8,128)(2,1)}, u32[]{:S(2)}, u32[]{:S(2)}) async-start(bf16[16,80,2048]{2,1,0:T(8,128)(2,1)} %bitcast.177), calls=%async_computation.3 | async-start | bytes 10485760 | tf_op jit(solution)/shard_map/all_to_all | solution.py:237
  1145.6 332.9 %all-gather.18.cloned.1.call-start = ((), (), s32[]{:S(2)}) async-start(), calls=%async_computation.10 | async-start | bytes 8912896 | tf_op jit(solution)/shard_map/all_gather | solution.py:267
  1277.1 12.2 copy-start.29
  1277.1 18.9 copy-start.34
  1289.3 15.4 copy-start.25
  1289.3 15.8 slice-start
  1296.0 9.1 slice-start.1
  1305.1 90.4 %copy-start.1 = (f32[128,2048]{1,0:T(8,128)}, f32[128,2048]{1,0:T(8,128)S(1)}, u32[]{:S(2)}) copy-start(f32[128,2048]{1,0:T(8,128)S(1)} %fusion.47) | copy-start | bytes 3145732
  1305.2 75.5 %copy-start.23 = (bf16[128,16,128]{2,0,1:T(8,128)(2,1)S(1)}, bf16[128,16,128]{2,0,1:T(8,128)(2,1)}, u32[]{:S(2)}) copy-start(bf16[128,16,128]{2,0,1:T(8,128)(2,1)} %maximum_convert_fusion.1) | copy-start | bytes 1572868
  1307.4 996.7 %reduce-scatter.2.cloned.1.call-start = ((), (), s32[]{:S(2)}) async-start(), calls=%async_computation.11 | async-start | bytes 35651584 | tf_op jit(solution)/shard_map/reduce_scatter | solution.py:312
  1380.7 14.9 copy-start.19
  1401.3 12.3 copy-start.14
  1401.3 12.3 copy-start.24
  1401.3 12.3 copy-start.48
  1490.7 10.6 copy-start.20
  1501.3 20.0 copy-start.6
  1501.3 15.7 copy-start.27
  1501.3 15.7 copy-start.32
  1519.3 20.0 copy-start.8
  1521.3 18.0 copy-start.10
  1598.2 814.6 %all-reduce.5.cloned.1.call-start = ((), (), s32[]{:S(2)}) async-start(), calls=%async_computation.12 | async-start | bytes 29360128 | tf_op jit(solution)/shard_map/psum | solution.py:329
  1598.2 10.5 copy-start.62
  1598.2 20.4 slice-start.2
  1608.7 9.9 slice-start.3
  1608.7 9.9 copy-start.63
  2307.5 5.4 copy-start.7
  2307.5 5.4 copy-start.9
  2307.6 5.4 copy-start.11
  2312.9 12.7 copy-start.39
  2312.9 97.3 %copy-start.55 = (f32[128]{0:T(128)S(1)}, f32[128]{0:T(128)}, u32[]{:S(2)}) copy-start(f32[128]{0:T(128)} %copy-done.54) | copy-start | bytes 1540
  2312.9 97.3 %copy-start.2 = (f32[128,2048]{1,0:T(8,128)S(1)}, f32[128,2048]{1,0:T(8,128)}, u32[]{:S(2)}) copy-start(f32[128,2048]{1,0:T(8,128)} %copy-done.1) | copy-start | bytes 3145732
  2412.7 5.9 copy-start.17
  2415.0 8.0 copy-start.16
  2423.0 4.4 copy-start.15
  (15 other events, 36.2 us)
Sparse Core Ops, SparseCore 0:
  10.8 272.0 all-gather.7
  303.2 140.5 all-gather.11
  446.5 110.6 all-gather.9
  559.8 111.0 all-gather.13
  964.1 279.6 all-gather.15
  1307.5 127.2 all-gather.17
  1598.3 705.7 reduce-scatter.1
  2309.7 60.0 all-reduce.4
where the time goes:
time: 2450 us; the launch traced here: 2440 us
  waiting for transfers between devices  1570 us (64%)
  blocking collectives  313 us (13%)
  matrix products  235 us (10%)
  local copies, waits for them, and re-layouts  128 us (5%)
  other arithmetic  98.8 us (4%)
  starting transfers between devices  72.2 us (3%)
    reduce_scatter x1, waiting for transfers between devices, per_device(): lax.psum_scatter(jnp.concatenate([qkv_rows.reshape(lax.axis_size('dp') *...  678 us
    all_gather x1, waiting for transfers between devices, per_device(): lax.all_gather(qkv_weight, 'dp', axis=0, tiled=True)  271 us
    all_to_all x1, waiting for transfers between devices, per_device(): lax.all_to_all(ungroup(expert_out, devices, local_experts, slot_most), 'd...  120 us
    all_to_all x1, waiting for transfers between devices, per_device(): lax.all_to_all(ungroup(row_grad, devices, local_experts, slot_most), 'dp'...  119 us
    all_to_all x1, blocking collectives, per_device(): lax.all_to_all(outbox, 'dp', split_axis=0, concat_axis=0, tiled=True)  119 us
    all_gather x1, waiting for transfers between devices, per_device(): lax.all_gather(out_weight, 'dp', axis=0, tiled=True)  102 us
    all_gather x1, waiting for transfers between devices, per_device(): lax.all_gather(values_own, 'dp', axis=0, tiled=True)  101 us
    all_gather x1, waiting for transfers between devices, per_device(): lax.all_gather(keys_own, 'dp', axis=0, tiled=True)  97 us
  transfers between devices with their start and end apart: 11, of which 8 were waited for; matrix products, arithmetic and copies ran while one was open for 10% of the time, Pallas kernels for 0%

commit v1 on v0

v1 whole, which is shorter than its diff:
```python
import functools

import jax
import jax.numpy as jnp
import numpy as np
from jax import lax
from jax.experimental import pallas as pl
from jax.experimental.pallas import tpu as pltpu
from jax.sharding import PartitionSpec as P

H = 16
HD = 128
TOPK = 8
EPS = 1e-06
THETA = 50000.0
MESH = pl.DeviceIdType.MESH
MIB = 2**20
BF = jnp.bfloat16
F32 = jnp.float32
SCALE = HD**-0.5
LOG2E = 1.4426950408889634


def places():
    me = lax.axis_index("dp")
    z, y, x = me // 4, (me // 2) % 2, me % 2
    xor = [z, z + 1 - 2 * (z % 2), (z + 2) % 4, 3 - z]
    at = lambda k, yy, xx: xor[k] * 4 + yy * 2 + xx
    return dict(
        me=me,
        col=[at(k, y, x) for k in range(4)],
        X=[at(k, y, 1 - x) for k in range(4)],
        Y=[at(k, 1 - y, x) for k in range(4)],
        D=[at(k, 1 - y, 1 - x) for k in range(4)],
    )


def barrier(targets, pair=False):
    sem = pltpu.get_barrier_semaphore()
    for t in targets:
        pl.semaphore_signal(sem, inc=1, device_id={"dp": t}, device_id_type=MESH)
    count = len(targets)
    if pair:
        pl.semaphore_signal(sem, inc=1, device_id={"grp": partner()}, device_id_type=MESH)
        count += 1
    pl.semaphore_wait(sem, count)


def partner():
    g = lax.axis_index("grp")
    return g + 1 - 2 * (g % 2)


def push(src, dst, send, recv, to):
    c = pltpu.make_async_remote_copy(
        src_ref=src, dst_ref=dst, send_sem=send, recv_sem=recv,
        device_id={"dp": to}, device_id_type=MESH,
    )
    c.start()
    return c


def push_pair(src, dst, send, recv):
    c = pltpu.make_async_remote_copy(
        src_ref=src, dst_ref=dst, send_sem=send, recv_sem=recv,
        device_id={"grp": partner()}, device_id_type=MESH,
    )
    c.start()
    return c


GATHER_SEMS = [pltpu.SemaphoreType.DMA((4,))] * 6 + [pltpu.SemaphoreType.DMA((4, 2))] * 2 + [pltpu.SemaphoreType.DMA]


def gather_steps(src, dst, rows, sems):
    zs, zr, xs, xr, ys, yr, ds, dr, own = sems
    p = places()
    half = rows // 2
    blk = lambda b: dst.at[pl.ds(pl.multiple_of(b * rows, rows), rows)]
    part = lambda b, h: dst.at[pl.ds(pl.multiple_of(b * rows + h * half, half), half)]
    me, xn, yn = p["me"], p["X"][0], p["Y"][0]
    mine = pltpu.make_async_copy(src, blk(me), own)
    mine.start()
    xc = [push(src, blk(me), xs.at[0], xr.at[0], xn)]
    yc = [push(src, blk(me), ys.at[0], yr.at[0], yn)]
    zc = [push(src, blk(me), zs.at[k], zr.at[k], p["col"][k]) for k in (1, 2, 3)]
    dc = []
    mine.wait()
    yield
    for k in range(4):
        if k < 3:
            zc[k].wait_recv()
            b = p["col"][k + 1]
            xc.append(push(blk(b), blk(b), xs.at[k + 1], xr.at[k + 1], xn))
            yc.append(push(blk(b), blk(b), ys.at[k + 1], yr.at[k + 1], yn))
        xc[k].wait_recv()
        dc.append(push(part(p["X"][k], 0), part(p["X"][k], 0), ds.at[k, 0], dr.at[k, 0], yn))
        yc[k].wait_recv()
        dc.append(push(part(p["Y"][k], 1), part(p["Y"][k], 1), ds.at[k, 1], dr.at[k, 1], xn))
        yield
    for c in dc:
        c.wait_recv()
    for c in xc + yc + zc + dc:
        c.wait_send()


def gather_targets():
    p = places()
    return [p["col"][1], p["col"][2], p["col"][3], p["X"][0], p["Y"][0]]


def run(*steps):
    live = list(steps)
    while live:
        for s in list(live):
            try:
                next(s)
            except StopIteration:
                live.remove(s)


SCATTER_SEMS = [pltpu.SemaphoreType.DMA((4, 2))] * 2 + [pltpu.SemaphoreType.DMA((4,))] * 6


def scatter_bufs(rows, width):
    return [
        pltpu.VMEM((8, rows // 2, width), BF),
        pltpu.VMEM((4, rows, width), BF),
        pltpu.VMEM((4, rows, width), BF),
        pltpu.VMEM((4, rows, width), BF),
    ]


def scatter_sum(part, out, rows, bufs, sems):
    rd, rx, ry, rz = bufs
    ds, dr, xs, xr, ys, yr, zs, zr = sems
    p = places()
    half = rows // 2
    xn, yn = p["X"][0], p["Y"][0]
    order = (1, 2, 3, 0)
    sent = []
    da, db, xc, yc, zc = {}, {}, {}, {}, {}
    for k in order:
        b = p["D"][k]
        da[k] = push(part.at[b, pl.ds(0, half)], rd.at[2 * k], ds.at[k, 0], dr.at[k, 0], yn)
        db[k] = push(part.at[b, pl.ds(half, half)], rd.at[2 * k + 1], ds.at[k, 1], dr.at[k, 1], xn)
    for k in order:
        b = p["X"][k]
        da[k].wait_recv()
        part[b, pl.ds(0, half)] = (part[b, pl.ds(0, half)].astype(F32) + rd[2 * k].astype(F32)).astype(BF)
        xc[k] = push(part.at[b], rx.at[k], xs.at[k], xr.at[k], xn)
        b = p["Y"][k]
        db[k].wait_recv()
        part[b, pl.ds(half, half)] = (part[b, pl.ds(half, half)].astype(F32) + rd[2 * k + 1].astype(F32)).astype(BF)
        yc[k] = push(part.at[b], ry.at[k], ys.at[k], yr.at[k], yn)
    for k in order:
        b = p["col"][k]
        xc[k].wait_recv()
        yc[k].wait_recv()
        total = part[b].astype(F32) + rx[k].astype(F32) + ry[k].astype(F32)
        if k:
            part[b] = total.astype(BF)
            zc[k] = push(part.at[b], rz.at[k], zs.at[k], zr.at[k], b)
        else:
            out[...] = total
    for k in (1, 2, 3):
        zc[k].wait_recv()
        out[...] += rz[k].astype(F32)
    for group in (da, db, xc, yc, zc):
        for c in group.values():
            c.wait_send()


ANY = pl.BlockSpec(memory_space=pl.ANY)
VM = pl.BlockSpec(memory_space=pltpu.VMEM)


def params(cid, vmem=60):
    return pltpu.CompilerParams(collective_id=cid, has_side_effects=True, vmem_limit_bytes=vmem * MIB)


def front_kernel(n_ref, m_ref, w_ref, nall, mall, wh, *sems):
    g_sems, (ms, mr, mo, ws, wr, ps, pr, wo) = sems[:9], sems[9:]
    me = lax.axis_index("dp")
    core = lax.axis_index("grp") % 2
    barrier([lax.rem(me + d, 16) for d in range(1, 16)], pair=True)
    hr = HD // 2
    g = gather_steps(n_ref, nall, n_ref.shape[0], g_sems)
    next(g)
    own = pltpu.make_async_copy(m_ref, mall.at[me], mo)
    own.start()
    mc = []
    for d in range(1, 16):
        to = lax.rem(me + d, 16)
        mc.append(push(m_ref, mall.at[me], ms.at[d], mr.at[d], to))
    off = core * hr
    for l in range(3):
        b = 3 * me + l
        to, slot = lax.rem(b, 16), b // 16
        src = w_ref.at[pl.ds(pl.multiple_of(l * HD + off, hr), hr)]
        dst = wh.at[pl.ds(pl.multiple_of(slot * HD + off, hr), hr)]

        @pl.when(to != me)
        def _():
            push(src, dst, ws.at[l], wr.at[slot], to)

        @pl.when(to == me)
        def _():
            pltpu.make_async_copy(src, dst, wr.at[slot]).start()

    for s in range(3):
        dst = wh.at[pl.ds(pl.multiple_of(s * HD + off, hr), hr)]
        pltpu.make_async_copy(dst, dst, wr.at[s]).wait()
        push_pair(dst, dst, ps.at[s], pr.at[s])
    for _ in g:
        pass
    own.wait()
    for c in mc:
        c.wait()
    for l in range(3):
        b = 3 * me + l
        src = w_ref.at[pl.ds(pl.multiple_of(l * HD + off, hr), hr)]

        @pl.when(lax.rem(b, 16) != me)
        def _():
            pltpu.make_async_copy(src, src, ws.at[l]).wait()

    for s in range(3):
        dst = wh.at[pl.ds(pl.multiple_of(s * HD + off, hr), hr)]
        other = wh.at[pl.ds(pl.multiple_of(s * HD + (hr - off), hr), hr)]
        pltpu.make_async_copy(dst, dst, ps.at[s]).wait()
        pltpu.make_async_copy(other, other, pr.at[s]).wait()


def front(normed, meta, w):
    rows, width = normed.shape
    return pl.pallas_call(
        front_kernel,
        out_shape=[
            jax.ShapeDtypeStruct((16 * rows, width), BF),
            jax.ShapeDtypeStruct((16,) + meta.shape, F32),
            jax.ShapeDtypeStruct((3 * HD, width), BF),
        ],
        in_specs=[ANY] * 3,
        out_specs=[ANY] * 3,
        scratch_shapes=GATHER_SEMS
        + [pltpu.SemaphoreType.DMA((16,)), pltpu.SemaphoreType.DMA((16,)), pltpu.SemaphoreType.DMA]
        + [pltpu.SemaphoreType.DMA((3,))] * 4
        + [pltpu.SemaphoreType.DMA],
        compiler_params=params(0),
        name="front",
    )(normed, meta, w)


def gather_kernel(x_ref, o_ref, *sems):
    barrier(gather_targets())
    run(gather_steps(x_ref, o_ref, x_ref.shape[0], sems))


def gather(x, cid):
    rows, width = x.shape
    return pl.pallas_call(
        gather_kernel,
        out_shape=jax.ShapeDtypeStruct((16 * rows, width), x.dtype),
        in_specs=[ANY],
        out_specs=ANY,
        scratch_shapes=GATHER_SEMS,
        compiler_params=params(cid),
        name=f"gather_{cid}",
    )(x)


def scatter_kernel(p_ref, o_ref, part, load, *rest):
    bufs, sems = rest[:4], rest[4:]
    c = pltpu.make_async_copy(p_ref, part, load)
    c.start()
    barrier(gather_targets())
    c.wait()
    scatter_sum(part, o_ref, part.shape[1], bufs, sems)


def scatter(x, cid):
    rows, width = x.shape[0] // 16, x.shape[1]
    return pl.pallas_call(
        scatter_kernel,
        out_shape=jax.ShapeDtypeStruct((rows, width), F32),
        in_specs=[ANY],
        out_specs=VM,
        scratch_shapes=[pltpu.VMEM((16, rows, width), BF), pltpu.SemaphoreType.DMA]
        + scatter_bufs(rows, width)
        + SCATTER_SEMS,
        compiler_params=params(cid),
        name=f"scatter_{cid}",
    )(x.reshape(16, rows, width))


def swap_kernel(x_ref, o_ref, ss, rs, lo):
    me = lax.axis_index("dp")
    barrier([lax.rem(me + d, 16) for d in range(1, 16)])
    own = pltpu.make_async_copy(x_ref.at[me], o_ref.at[me], lo)
    own.start()
    sent = []
    for d in range(1, 16):
        to = lax.rem(me + d, 16)
        sent.append(push(x_ref.at[to], o_ref.at[me], ss.at[d], rs.at[d], to))
    own.wait()
    for c in sent:
        c.wait()


def swap(x, cid):
    return pl.pallas_call(
        swap_kernel,
        out_shape=jax.ShapeDtypeStruct(x.shape, x.dtype),
        in_specs=[ANY],
        out_specs=ANY,
        scratch_shapes=[pltpu.SemaphoreType.DMA((16,))] * 2 + [pltpu.SemaphoreType.DMA],
        compiler_params=params(cid),
        name=f"swap_{cid}",
    )(x)


def return_kernel(x_ref, o_ref, ss, rs):
    me = lax.axis_index("dp")
    barrier([lax.rem(me + d, 16) for d in range(1, 16)])
    for s in range(3):
        b = 16 * s + me
        to, slot = b // 3, lax.rem(b, 3)

        @pl.when(to != me)
        def _():
            push(x_ref.at[s], o_ref.at[slot], ss.at[s], rs.at[slot], to)

        @pl.when(to == me)
        def _():
            pltpu.make_async_copy(x_ref.at[s], o_ref.at[slot], rs.at[slot]).start()

    for s in range(3):
        pltpu.make_async_copy(x_ref.at[s], o_ref.at[s], rs.at[s]).wait()

        @pl.when((16 * s + me) // 3 != me)
        def _():
            pltpu.make_async_copy(x_ref.at[s], o_ref.at[s], ss.at[s]).wait()


def give_back(x, cid):
    return pl.pallas_call(
        return_kernel,
        out_shape=jax.ShapeDtypeStruct(x.shape, x.dtype),
        in_specs=[ANY],
        out_specs=ANY,
        scratch_shapes=[pltpu.SemaphoreType.DMA((3,))] * 2,
        compiler_params=params(cid),
        name="give_back",
    )(x)


QB = 256


def attend_kernel(q, k, v, sq, sk, ctx, lse):
    s = lax.dot_general(q[...], k[...], (((1,), (1,)), ((), ())), preferred_element_type=F32)
    s = jnp.where(sq[...] == sk[...], s, -1e30)
    peak = jnp.maximum(jnp.max(s, -1, keepdims=True), -1e29)
    ex = jnp.exp2((s - peak) * (SCALE * LOG2E))
    total = jnp.maximum(jnp.sum(ex, -1, keepdims=True), 1.0)
    prob = (ex * (1.0 / total)).astype(BF)
    ctx[...] = jnp.dot(prob, v[...], preferred_element_type=F32).astype(BF)
    lse[...] = peak * (SCALE * LOG2E) + jnp.log2(total)


def attend(q, k, v, sq, sk):
    n = q.shape[0]
    row = lambda w: pl.BlockSpec((QB, w), lambda i: (i, 0))
    full = lambda r, w: pl.BlockSpec((r, w), lambda i: (0, 0))
    return pl.pallas_call(
        attend_kernel,
        grid=(n // QB,),
        out_shape=[jax.ShapeDtypeStruct((n, HD), BF), jax.ShapeDtypeStruct((n, 1), F32)],
        in_specs=[row(HD), full(n, HD), full(n, HD), row(1), full(1, n)],
        out_specs=[row(HD), row(1)],
        compiler_params=pltpu.CompilerParams(vmem_limit_bytes=48 * MIB),
        name="attend",
    )(q, k, v, sq, sk)


def attend_back_kernel(q, k, v, sq, sk, lse, dc, dq, dkt, dvt):
    @pl.when(pl.program_id(0) == 0)
    def _():
        dkt[...] = jnp.zeros_like(dkt)
        dvt[...] = jnp.zeros_like(dvt)

    s = lax.dot_general(q[...], k[...], (((1,), (1,)), ((), ())), preferred_element_type=F32)
    prob = jnp.where(sq[...] == sk[...], jnp.exp2(s * (SCALE * LOG2E) - lse[...]), 0.0)
    dp = lax.dot_general(dc[...], v[...], (((1,), (1,)), ((), ())), preferred_element_type=F32)
    delta = jnp.sum(prob * dp, -1, keepdims=True)
    ds = (prob * (dp - delta)).astype(BF)
    dq[...] = jnp.dot(ds, k[...], preferred_element_type=F32) * SCALE
    dkt[...] += lax.dot_general(q[...], ds, (((0,), (0,)), ((), ())), preferred_element_type=F32) * SCALE
    dvt[...] += lax.dot_general(dc[...], prob.astype(BF), (((0,), (0,)), ((), ())), preferred_element_type=F32)


def attend_back(q, k, v, sq, sk, lse, dc):
    n = q.shape[0]
    row = lambda w: pl.BlockSpec((QB, w), lambda i: (i, 0))
    full = lambda r, w: pl.BlockSpec((r, w), lambda i: (0, 0))
    return pl.pallas_call(
        attend_back_kernel,
        grid=(n // QB,),
        out_shape=[jax.ShapeDtypeStruct((n, HD), F32), jax.ShapeDtypeStruct((HD, n), F32), jax.ShapeDtypeStruct((HD, n), F32)],
        in_specs=[row(HD), full(n, HD), full(n, HD), row(1), full(1, n), row(1), row(HD)],
        out_specs=[row(HD), full(HD, n), full(HD, n)],
        compiler_params=pltpu.CompilerParams(vmem_limit_bytes=48 * MIB),
        name="attend_back",
    )(q, k, v, sq, sk, lse, dc)


def rmsnorm(field, gain_row):
    return field * lax.rsqrt(jnp.mean(field * field, -1, keepdims=True) + EPS) * gain_row


def rotate(field, cos_table, sin_table):
    half = field.shape[-1] // 2
    first, second = field[..., :half], field[..., half:]
    return jnp.concatenate(
        [first * cos_table - second * sin_table, second * cos_table + first * sin_table], -1
    )


def rotary_tables(length):
    position = jnp.arange(length).astype(F32)
    freq = THETA ** (-(jnp.arange(HD // 2).astype(F32) * 2.0 / HD))
    angle = position[:, None] * freq[None, :]
    return jnp.cos(angle), jnp.sin(angle)


def dot(a, b, ca, cb):
    return lax.dot_general(a, b, (((ca,), (cb,)), ((), ())), preferred_element_type=F32)


def per_device(
    tokens, segments, routes, route_weight, capacity, norm_gain,
    qkv_weight, out_weight, gate_weight, up_weight, down_weight, cotangent,
):
    rows, width = tokens.shape
    seq = segments.shape[0]
    me = lax.axis_index("dp")
    slots = 80
    stream = tokens.astype(F32)
    normed = rmsnorm(stream, norm_gain[0]).astype(BF)
    meta = jnp.concatenate([routes.astype(F32).T, route_weight.T], 0)
    normed_all, meta_all, w_head = front(normed, meta, qkv_weight)
    projected = dot(normed_all, w_head, 1, 1)
    cos_table, sin_table = rotary_tables(seq)
    q = rotate(projected[:, :HD], cos_table, sin_table).astype(BF)
    k = rotate(projected[:, HD : 2 * HD], cos_table, sin_table).astype(BF)
    v = projected[:, 2 * HD :].astype(BF)
    sq = segments[:, None]
    sk = jnp.where(segments == 0, -1, segments)[None, :]
    ctx_h, lse = attend(q, k, v, sq, sk)
    context = swap(ctx_h.reshape(16, rows, HD), 1).transpose(1, 0, 2).reshape(rows, width)
    dense_out = gather(out_weight, 2)
    attended = dot(context, dense_out, 1, 1)
    middle = stream + attended
    normed2 = rmsnorm(middle, norm_gain[1]).astype(BF)
    normed2_all = gather(normed2, 3)
    cot_all = gather(cotangent, 4)
    mine = meta_all[:, :TOPK] == me.astype(F32)
    member = jnp.sum(mine.astype(F32), 1)
    weight = jnp.sum(jnp.where(mine, meta_all[:, TOPK:], 0.0), 1)
    local = jnp.cumsum(member, 1) - member
    before = jnp.cumsum(jnp.sum(member, 1)) - jnp.sum(member, 1)
    kept = (member > 0) & (local + before[:, None] < capacity[0].astype(F32))
    pick = (jnp.arange(slots, dtype=F32)[None, :, None] == local[:, None, :]) & kept[:, None, :]
    slot_weight = jnp.sum(jnp.where(pick, weight[:, None, :], 0.0), 2).reshape(16 * slots, 1)
    pick = pick.astype(BF)
    take = lambda a: jnp.einsum("jst,jtd->jsd", pick, a.reshape(16, rows, width), preferred_element_type=F32).reshape(16 * slots, width)
    put = lambda a: jnp.einsum("jst,jsd->jtd", pick, a.reshape(16, slots, width), preferred_element_type=F32).reshape(seq, width).astype(BF)
    xr = take(normed2_all).astype(BF)
    pg = (take(cot_all) * slot_weight).astype(BF)
    gate = dot(xr, gate_weight[0], 1, 0)
    up = dot(xr, up_weight[0], 1, 0)
    sig = jax.nn.sigmoid(gate)
    hidden = (gate * sig * up).astype(BF)
    eo = dot(hidden, down_weight[0], 1, 0).astype(BF)
    mix_part = put((eo.astype(F32) * slot_weight).astype(BF))
    hg = dot(pg, down_weight[0], 1, 1)
    gg = (hg * up * sig * (1.0 + gate * (1.0 - sig))).astype(BF)
    ug = (hg * gate * sig).astype(BF)
    rg = (dot(gg, gate_weight[0], 1, 1) + dot(ug, up_weight[0], 1, 1)).astype(BF)
    back_part = put(rg)
    down_g = dot(hidden, pg, 0, 0)
    gate_g = dot(xr, gg, 0, 0)
    up_g = dot(xr, ug, 0, 0)
    mixture = scatter(mix_part, 5)
    n2g = scatter(back_part, 6)
    layer = middle + mixture
    own_seg = lax.dynamic_slice_in_dim(segments, me * rows, rows)
    valid = (own_seg != 0).astype(F32)
    sums = jnp.stack(
        [
            jnp.sum(valid * jnp.sum(layer * layer, -1)),
            jnp.sum(valid * jnp.sum(attended * attended, -1)),
            jnp.sum(valid * jnp.sum(mixture * mixture, -1)),
            jnp.sum(valid) * width,
        ]
    )
    grad = cotangent.astype(F32)
    mg, gain2 = jax.vjp(rmsnorm, middle, norm_gain[1])[1](n2g)
    middle_grad = grad + mg
    attended_grad = middle_grad.astype(BF)
    context_grad = dot(attended_grad, dense_out, 1, 0).astype(BF)
    cg_h = swap(context_grad.reshape(rows, H, HD).transpose(1, 0, 2), 7).reshape(seq, HD)
    dq, dkt, dvt = attend_back(q, k, v, sq, sk, lse, cg_h)
    pgrad = jnp.concatenate(
        [rotate(dq, cos_table, -sin_table), rotate(dkt.T, cos_table, -sin_table), dvt.T], 1
    ).astype(BF)
    qkv_part = dot(pgrad, normed_all, 0, 0)
    qkv_sum = lax.psum(qkv_part.astype(BF), "grp")
    qkv_total = give_back(qkv_sum.reshape(3, HD, width), 8).reshape(3 * HD, width).astype(F32)
    normed_grad = scatter(dot(pgrad, w_head, 1, 0).astype(BF), 9)
    out_part = scatter(dot(attended_grad, context, 0, 0).astype(BF), 10)
    sg, gain1 = jax.vjp(rmsnorm, stream, norm_gain[0])[1](normed_grad)
    tokens_grad = middle_grad + sg
    seq_sums, gain_dp = lax.psum((sums, jnp.stack([gain1, gain2])), "dp")
    stat_row = jnp.sqrt(seq_sums[:3] / seq_sums[3]).reshape(1, 3)
    over = lambda a: lax.psum(a.astype(BF), "grp").astype(F32)
    return (
        layer.astype(BF),
        tokens_grad,
        qkv_total,
        over(out_part),
        over(gate_g)[None],
        over(up_g)[None],
        over(down_g)[None],
        over(gain_dp),
        stat_row,
    )


def solution(mesh):
    both = ("grp", "dp")
    in_specs = (
        P(both, None), P("grp"), P(both, None), P(both, None), P(), P(),
        P("dp", None), P("dp", None), P("dp", None, None), P("dp", None, None), P("dp", None, None),
        P(both, None),
    )
    out_specs = (
        P(both, None), P(both, None), P("dp", None), P("dp", None),
        P("dp", None, None), P("dp", None, None), P("dp", None, None), P(), P("grp", None),
    )
    return jax.shard_map(per_device, mesh=mesh, in_specs=in_specs, out_specs=out_specs, check_vma=False)
```

time: 2450 us -> 1160 us (0.47)
  waiting for transfers between devices: 1570 us -> 0.02 us
  Pallas kernels: 0 us -> 830 us
  blocking collectives: 313 us -> 80.9 us
  local copies, waits for them, and re-layouts: 128 us -> 18 us
  matrix products: 235 us -> 148 us
  starting transfers between devices: 72.2 us -> 0.04 us
  other arithmetic: 98.8 us -> 58.1 us
    pallas_call x0 -> x13, Pallas kernels: none -> 830 us  [the longest x4 361 us: scatter(): pl.pallas_call(scatter_kernel, out_shape=jax.ShapeDtypeStruct((rows, widt...]
    reduce_scatter x1 -> x0, waiting for transfers between devices: 678 us -> none  [per_device(): lax.psum_scatter(jnp.concatenate([qkv_rows.reshape(lax.axis_size('dp') *...]
    all_gather x6 -> x0, waiting for transfers between devices: 572 us -> none  [the longest x1 271 us: per_device(): lax.all_gather(qkv_weight, 'dp', axis=0, tiled=True)]
    all_to_all x3 -> x0, waiting for transfers between devices: 324 us -> none  [the longest x1 120 us: per_device(): lax.all_to_all(ungroup(expert_out, devices, local_experts, slot_most), 'd...]
    all_to_all x1 -> x0, blocking collectives: 119 us -> none  [per_device(): lax.all_to_all(outbox, 'dp', split_axis=0, concat_axis=0, tiled=True)]
    all_gather x3 -> x0, blocking collectives: 103 us -> none  [the longest x1 41.1 us: per_device(): lax.all_gather(row_total[:, :, 0].T, 'dp', axis=0, tiled=True)]
    dot_general x22 -> x19, matrix products: 235 us -> 148 us  [the longest x15 121 us: dot(): lax.dot_general(a, b, (((ca,), (cb,)), ((), ())), preferred_element_type=...]
    all_to_all x3 -> x0, starting transfers between devices: 71.9 us -> none  [the longest x1 47.7 us: per_device(): lax.all_to_all(ungroup(row_grad, devices, local_experts, slot_most), 'dp'...]
  transfers between devices with their start and end apart: 11 -> 1, of which waited for: 8 -> 0; matrix products, arithmetic and copies ran while one was open for 10% -> 1% of each run, Pallas kernels for 0% -> 9%
where the time goes in v1:
time: 1160 us; the launch traced here: 1150 us
  Pallas kernels  830 us (72%)
  matrix products  148 us (13%)
  blocking collectives  80.9 us (7%)
  other arithmetic  58.1 us (5%)
  local copies, waits for them, and re-layouts  18 us (2%)
  between operations  16.3 us (1%)
    pallas_call x4, Pallas kernels, scatter(): pl.pallas_call(scatter_kernel, out_shape=jax.ShapeDtypeStruct((rows, widt...  361 us
    pallas_call x3, Pallas kernels, gather(): pl.pallas_call(gather_kernel, out_shape=jax.ShapeDtypeStruct((16 * rows,...  252 us
    pallas_call x1, Pallas kernels, front(): pl.pallas_call(front_kernel, out_shape=[jax.ShapeDtypeStruct((16 * rows,...  127 us
    dot_general x15, matrix products, dot(): lax.dot_general(a, b, (((ca,), (cb,)), ((), ())), preferred_element_type=...  121 us
    psum x1, blocking collectives, per_device(): seq_sums, gain_dp = lax.psum((sums, jnp.stack([gain1, gain2])), 'dp')  64.4 us
    pallas_call x2, Pallas kernels, swap(): pl.pallas_call(swap_kernel, out_shape=jax.ShapeDtypeStruct(x.shape, x.dty...  35.5 us
    pallas_call x1, Pallas kernels, give_back(): pl.pallas_call(return_kernel, out_shape=jax.ShapeDtypeStruct(x.shape, x.d...  29.3 us
  transfers between devices with their start and end apart: 1, of which 0 were waited for; matrix products, arithmetic and copies ran while one was open for 1% of the time, Pallas kernels for 9%

profile of v1, /device:TPU:5, one launch (start us, length us, event | category | flops | bytes accessed | tf_op | source)
XLA Modules:
  0.0 1151.8 jit_solution(5871974133242131300)
XLA Ops:
  7.9 1.2 fusion.50
  11.9 1.1 copy.54.sq
  13.0 86.0 %gather_2.1 = bf16[2048,2048]{1,0:T(8,128)(2,1)} custom-call(bf16[128,2048]{1,0:T(8,128)(2,1)} %x_ref.2), custom_call_target="tpu_custom_call" | custom-call | tf_op jit(solution)/shard_map/gather_2/pallas_call | solution.py:262
  99.0 81.1 %gather_4.1 = bf16[2048,2048]{1,0:T(8,128)(2,1)} custom-call(bf16[128,2048]{1,0:T(8,128)(2,1)} %x_ref.3), custom_call_target="tpu_custom_call" | custom-call | tf_op jit(solution)/shard_map/gather_4/pallas_call | solution.py:262
  180.8 1.0 fusion.30.n_ref
  181.7 127.1 %front.1 = (bf16[2048,2048]{1,0:T(8,128)(2,1)}, f32[16,16,128]{2,1,0:T(8,128)}, bf16[384,2048]{1,0:T(8,128)(2,1)}) custom-call(bf16[128,2048]{1,0:T(8,128)(2,1)} %fusion.30.n_ref, f32[16,128]{1,0:T(8,128)} %pad_maximum_fusion.3.m_ref, bf16[384,2048]{1,0:T(8,128)(2,1)} %w_ref.1), custom_call_target="tpu_custom_call" | custom-call | tf_op jit(solution)/shard_map/front/pallas_call | solution.py:237
  308.9 1.1 select_reduce_fusion.1
  311.0 7.5 fusion.72
  318.6 5.1 fusion.45
  324.3 10.6 attend.1
  335.0 1.0 copy-done.11
  336.7 13.4 %swap_1.1 = bf16[16,128,128]{2,1,0:T(8,128)(2,1)} custom-call(bf16[16,128,128]{2,1,0:T(8,128)(2,1)} %bitcast.93), custom_call_target="tpu_custom_call" | custom-call | tf_op jit(solution)/shard_map/swap_1/pallas_call | solution.py:312
  350.1 1.3 copy.55
  351.4 6.9 multiply_reduce_fusion.5
  358.3 10.7 multiply_convert_fusion
  370.0 85.2 %gather_3.1 = bf16[2048,2048]{1,0:T(8,128)(2,1)} custom-call(bf16[128,2048]{1,0:T(8,128)(2,1)} %multiply_convert_fusion.5.x_ref), custom_call_target="tpu_custom_call" | custom-call | tf_op jit(solution)/shard_map/gather_3/pallas_call | solution.py:262
  455.3 5.0 convolution_convert_fusion.5
  460.4 7.5 fusion.5
  467.9 7.3 fusion.9
  475.2 13.0 %multiply_convert_fusion.2 = (bf16[1280,1024]{1,0:T(8,128)(2,1)}, bf16[1280,1024]{1,0:T(8,128)(2,1)}, bf16[1280,1024]{1,0:T(8,128)(2,1)S(1)}) fusion(f32[1280,1024]{1,0:T(8,128)} %fusion.9, f32[1280,1024]{1,0:T(8,128)} %fusion.5, bf16[1280,2048]{1,0:T(8,128)(2,1)S(1)} %bitcast.103, bf16[1,1024,2048]{2,1,0:T(8,128)(2,1)} %param.22), kind=kOutput, calls=%fused_computation.10 | convolution fusion | flops 5389680640 | bytes 27787264 | tf_op jit(solution)/shard_map/dot_general | solution.py:438
  488.2 10.1 convert_bitcast_fusion.2
  498.2 8.6 fusion.7
  506.9 7.5 convert_bitcast_fusion.1
  514.4 5.8 multiply_convert_fusion.1
  520.2 5.8 convolution_convert_fusion.4.p_ref
  526.0 83.5 %scatter_5.1 = f32[128,2048]{1,0:T(8,128)} custom-call(bf16[16,128,2048]{2,1,0:T(8,128)(2,1)} %convolution_convert_fusion.4.p_ref), custom_call_target="tpu_custom_call" | custom-call | tf_op jit(solution)/shard_map/scatter_5/pallas_call | solution.py:284
  609.5 10.1 add_convert_fusion
  619.6 5.8 convolution_convert_fusion.3.p_ref
  625.4 94.2 %scatter_6.1 = f32[128,2048]{1,0:T(8,128)} custom-call(bf16[16,128,2048]{2,1,0:T(8,128)(2,1)} %convolution_convert_fusion.3.p_ref), custom_call_target="tpu_custom_call" | custom-call | tf_op jit(solution)/shard_map/scatter_6/pallas_call | solution.py:284
  719.7 2.3 multiply_reduce_fusion.2
  722.0 1.5 fusion.48
  723.6 5.0 convolution_convert_fusion.7
  728.6 5.8 convolution_convert_fusion.2
  734.4 3.0 fusion
  737.4 10.4 convert_bitcast_fusion
  748.1 1.0 copy.58
  749.1 22.1 %swap_7.1 = bf16[16,128,128]{2,1,0:T(8,128)(2,1)} custom-call(bf16[16,128,128]{2,1,0:T(8,128)(2,1)} %bitcast.116), custom_call_target="tpu_custom_call" | custom-call | tf_op jit(solution)/shard_map/swap_7/pallas_call | solution.py:312
  771.3 1.0 copy-done.7
  772.3 14.7 %attend_back.1 = (f32[2048,128]{1,0:T(8,128)S(1)}, f32[128,2048]{1,0:T(8,128)S(1)}, f32[128,2048]{1,0:T(8,128)S(1)}) custom-call(bf16[2048,128]{1,0:T(8,128)(2,1)S(1)} %copy-done.4, bf16[2048,128]{1,0:T(8,128)(2,1)S(1)} %copy-done.6, bf16[2048,128]{1,0:T(8,128)(2,1)S(1)} %copy-done.2, s32[2048,1]{1,0:T(8,128)} %copy-done, s32[1,2048]{1,0:T(1,128)S(1)} %bitcast.95, ...), custom_call_target="tpu_custom_call" | custom-call | tf_op jit(solution)/shard_map/attend_back/pallas_call | solution.py:407
  787.0 1.0 copy-done.8
  788.0 1.0 copy-done.10
  789.0 2.5 copy.60
  791.5 8.0 fusion.39
  799.5 1.2 copy.64
  800.7 1.2 copy.63
  802.5 8.4 convolution_convert_fusion.6
  811.0 84.5 %scatter_10.1 = f32[128,2048]{1,0:T(8,128)} custom-call(bf16[16,128,2048]{2,1,0:T(8,128)(2,1)} %bitcast.100), custom_call_target="tpu_custom_call" | custom-call | tf_op jit(solution)/shard_map/scatter_10/pallas_call | solution.py:284
  895.5 2.1 convert_element_type.234
  897.6 1.4 copy-done.29
  899.4 7.0 convolution_convert_fusion
  906.5 98.3 %scatter_9.1 = f32[128,2048]{1,0:T(8,128)} custom-call(bf16[16,128,2048]{2,1,0:T(8,128)(2,1)} %bitcast.109), custom_call_target="tpu_custom_call" | custom-call | tf_op jit(solution)/shard_map/scatter_9/pallas_call | solution.py:284
  1004.8 1.4 select_reduce_fusion.4
  1006.9 2.0 pad_maximum_fusion.4
  1008.9 1.6 fusion.31
  1010.6 64.4 %all-reduce = (bf16[2,2048]{1,0:T(2,128)(2,1)S(1)}, f32[4]{0:T(128)S(1)}) all-reduce(f32[2,2048]{1,0:T(2,128)S(1)} %pad_maximum_fusion.2, f32[4]{0:T(128)S(1)} %pad_maximum_fusion.4), channel_id=1, replica_groups=mesh['grp'=2,'dp'=16] {'dp'}, use_global_device_ids=true, to_apply=%region_17.18 | all-reduce | flops 4100 | bytes 24608 | tf_op jit(solution)/shard_map/psum | solution.py:525
  1075.5 16.5 %psum.62 = bf16[2,2048]{1,0:T(2,128)(2,1)S(1)} all-reduce(bf16[2,2048]{1,0:T(2,128)(2,1)S(1)} %get-tuple-element.40), channel_id=1, replica_groups=mesh['grp'=2,'dp'=16] {'grp'}, use_global_device_ids=true, to_apply=%region_18.19 | all-reduce | flops 4096 | bytes 16384 | tf_op jit(solution)/shard_map/psum | solution.py:527
  1092.6 1.2 sqrt_bitcast_fusion
  1093.8 2.5 fusion.49
  1096.3 29.3 %give_back.1 = bf16[3,128,2048]{2,1,0:T(8,128)(2,1)} custom-call(bf16[3,128,2048]{2,1,0:T(8,128)(2,1)} %get-tuple-element.42.x_ref), custom_call_target="tpu_custom_call" | custom-call | tf_op jit(solution)/shard_map/give_back/pallas_call | solution.py:347
  1125.6 2.3 convert_element_type.235
  1127.9 3.4 bitcast_convert_fusion
  1131.3 4.4 broadcast_in_dim.70
  1135.8 4.4 broadcast_in_dim.72
  1140.2 4.4 broadcast_in_dim.74
  (132 shorter events, 9.5 us)
Async XLA Ops:
  7.2 1089.1 %all-reduce.4.cloned.1.call-start = ((), (), s32[]{:S(2)}) async-start(), calls=%async_computation | async-start | bytes 29360128 | tf_op jit(solution)/shard_map/psum | solution.py:519
  7.2 311.4 %copy-start.33 = (f32[64]{0:T(128)}, f32[64]{0:T(128)S(1)}, u32[]{:S(2)}) copy-start(f32[64]{0:T(128)S(1)} %negate_power_fusion) | copy-start | bytes 772
  7.3 311.4 %copy-start.26 = (f32[2048]{0:T(1024)}, f32[2048]{0:T(1024)S(1)}, u32[]{:S(2)}) copy-start(f32[2048]{0:T(1024)S(1)} %iota_convert_fusion) | copy-start | bytes 24580
  9.2 0.5 copy-start.36
  9.7 171.1 %copy-start.30 = (f32[128]{0:T(128)}, f32[128]{0:T(128)S(1)}, u32[]{:S(2)}) copy-start(f32[128]{0:T(128)S(1)} %fusion.69) | copy-start | bytes 1540
  11.1 313.2 %copy-start.13 = (s32[2048]{0:T(1024)}, s32[2048]{0:T(1024)S(1)}, u32[]{:S(2)}) copy-start(s32[2048]{0:T(1024)S(1)} %compare_select_fusion) | copy-start | bytes 24580
  11.9 168.9 %copy-start.24 = (f32[1,2048]{1,0:T(1,128)}, f32[1,2048]{1,0:T(1,128)S(1)}, u32[]{:S(2)}) copy-start(f32[1,2048]{1,0:T(1,128)S(1)} %get-tuple-element.65) | copy-start | bytes 24580
  13.0 311.4 %copy-start = (s32[2048,1]{1,0:T(8,128)}, s32[2048,1]{1,0:T(8,128)S(1)}, u32[]{:S(2)}) copy-start(s32[2048,1]{1,0:T(8,128)S(1)} %copy.54.sq) | copy-start | bytes 24580
  99.0 81.1 %copy-start.32 = (f32[128,8]{0,1:T(8,128)S(1)}, f32[128,8]{0,1:T(8,128)}, u32[]{:S(2)}) copy-start(f32[128,8]{0,1:T(8,128)} %param.15) | copy-start | bytes 12292
  99.0 81.8 %copy-start.17 = (bf16[128,2048]{1,0:T(8,128)(2,1)S(1)}, bf16[128,2048]{1,0:T(8,128)(2,1)}, u32[]{:S(2)}) copy-start(bf16[128,2048]{1,0:T(8,128)(2,1)} %param.12) | copy-start | bytes 1572868
  318.6 16.3 %copy-start.1 = (bf16[2048,128]{1,0:T(8,128)(2,1)}, bf16[2048,128]{1,0:T(8,128)(2,1)S(1)}, u32[]{:S(2)}) copy-start(bf16[2048,128]{1,0:T(8,128)(2,1)S(1)} %slice.96.v) | copy-start | bytes 1572868
  324.3 12.4 %copy-start.3 = (bf16[2048,128]{1,0:T(8,128)(2,1)}, bf16[2048,128]{1,0:T(8,128)(2,1)S(1)}, u32[]{:S(2)}) copy-start(bf16[2048,128]{1,0:T(8,128)(2,1)S(1)} %get-tuple-element.70.q) | copy-start | bytes 1572868
  324.3 12.4 %copy-start.5 = (bf16[2048,128]{1,0:T(8,128)(2,1)}, bf16[2048,128]{1,0:T(8,128)(2,1)S(1)}, u32[]{:S(2)}) copy-start(bf16[2048,128]{1,0:T(8,128)(2,1)S(1)} %get-tuple-element.71.k) | copy-start | bytes 1572868
  335.0 1.0 copy-start.11
  335.9 0.8 copy-start.12
  455.3 5.1 copy-start.40
  460.3 7.6 copy-start.38
  460.4 14.8 %slice-start.3 = ((s8[5242880]{0:T(1024)(128)(4,1)}), s8[4194304]{0:T(1024)(128)(4,1)S(1)}, s32[]{:S(2)}) async-start(s8[5242880]{0:T(1024)(128)(4,1)} %bitcast.101), calls=%async_computation.4 | async-start | bytes 8388608
  467.9 7.3 slice-start.4
  488.2 26.2 %copy-start.42 = (bf16[1280,1024]{1,0:T(8,128)(2,1)}, bf16[1280,1024]{1,0:T(8,128)(2,1)S(1)}, u32[]{:S(2)}) copy-start(bf16[1280,1024]{1,0:T(8,128)(2,1)S(1)} %get-tuple-element.53) | copy-start | bytes 7864324
  488.2 10.1 copy-start.44
  498.2 8.6 copy-start.43
  506.9 7.5 copy-start.39
  625.4 94.2 %copy-start.22 = (f32[128,2048]{1,0:T(8,128)S(1)}, f32[128,2048]{1,0:T(8,128)}, u32[]{:S(2)}) copy-start(f32[128,2048]{1,0:T(8,128)} %scatter_5.1) | copy-start | bytes 3145732
  625.4 96.6 %copy-start.23 = (bf16[128,2048]{1,0:T(8,128)(2,1)S(1)}, bf16[128,2048]{1,0:T(8,128)(2,1)}, u32[]{:S(2)}) copy-start(bf16[128,2048]{1,0:T(8,128)(2,1)} %x_ref.3) | copy-start | bytes 1572868
  723.5 5.1 copy-start.15
  723.5 10.9 slice-start
  723.5 10.9 slice-start.1
  728.6 5.8 slice-start.2
  737.4 33.8 %copy-start.2 = (bf16[2048,128]{1,0:T(8,128)(2,1)S(1)}, bf16[2048,128]{1,0:T(8,128)(2,1)}, u32[]{:S(2)}) copy-start(bf16[2048,128]{1,0:T(8,128)(2,1)} %copy-done.1) | copy-start | bytes 1572868
  737.4 33.8 %copy-start.4 = (bf16[2048,128]{1,0:T(8,128)(2,1)S(1)}, bf16[2048,128]{1,0:T(8,128)(2,1)}, u32[]{:S(2)}) copy-start(bf16[2048,128]{1,0:T(8,128)(2,1)} %copy-done.3) | copy-start | bytes 1572868
  737.4 33.8 %copy-start.6 = (bf16[2048,128]{1,0:T(8,128)(2,1)S(1)}, bf16[2048,128]{1,0:T(8,128)(2,1)}, u32[]{:S(2)}) copy-start(bf16[2048,128]{1,0:T(8,128)(2,1)} %copy-done.5) | copy-start | bytes 1572868
  737.4 33.8 %copy-start.14 = (s32[2048]{0:T(1024)S(1)}, s32[2048]{0:T(1024)}, u32[]{:S(2)}) copy-start(s32[2048]{0:T(1024)} %copy-done.13) | copy-start | bytes 24580
  747.8 43.7 %copy-start.27 = (f32[2048]{0:T(1024)S(1)}, f32[2048]{0:T(1024)}, u32[]{:S(2)}) copy-start(f32[2048]{0:T(1024)} %copy-done.26) | copy-start | bytes 24580
  747.8 43.7 %copy-start.34 = (f32[64]{0:T(128)S(1)}, f32[64]{0:T(128)}, u32[]{:S(2)}) copy-start(f32[64]{0:T(128)} %copy-done.33) | copy-start | bytes 772
  771.2 1.0 copy-start.7
  787.0 1.0 copy-start.8
  788.0 1.0 copy-start.10
  791.5 11.0 copy-start.9
  802.5 8.5 copy-start.28
  897.6 1.4 copy-start.29
  897.6 1.9 copy-start.41
  906.5 98.4 %copy-start.35 = (f32[128]{0:T(128)S(1)}, f32[128]{0:T(128)}, u32[]{:S(2)}) copy-start(f32[128]{0:T(128)} %get-tuple-element.63) | copy-start | bytes 1540
  906.5 102.4 %copy-start.18 = (bf16[128,2048]{1,0:T(8,128)(2,1)S(1)}, bf16[128,2048]{1,0:T(8,128)(2,1)}, u32[]{:S(2)}) copy-start(bf16[128,2048]{1,0:T(8,128)(2,1)} %param.12) | copy-start | bytes 1572868
  906.5 102.4 %copy-start.25 = (f32[1,2048]{1,0:T(1,128)S(1)}, f32[1,2048]{1,0:T(1,128)}, u32[]{:S(2)}) copy-start(f32[1,2048]{1,0:T(1,128)} %copy-done.24) | copy-start | bytes 24580
  906.5 102.4 %copy-start.31 = (f32[128]{0:T(128)S(1)}, f32[128]{0:T(128)}, u32[]{:S(2)}) copy-start(f32[128]{0:T(128)} %copy-done.30) | copy-start | bytes 1540
  906.5 187.3 %copy-start.37 = (f32[128]{0:T(128)S(1)}, f32[128]{0:T(128)}, u32[]{:S(2)}) copy-start(f32[128]{0:T(128)} %copy-done.36) | copy-start | bytes 1540
  906.5 187.3 %copy-start.16 = (f32[128,2048]{1,0:T(8,128)S(1)}, f32[128,2048]{1,0:T(8,128)}, u32[]{:S(2)}) copy-start(f32[128,2048]{1,0:T(8,128)} %copy-done.15) | copy-start | bytes 3145732
  1125.6 5.7 copy-start.21
  1131.3 4.4 copy-start.20
  1135.8 4.4 copy-start.19
Sparse Core Ops, SparseCore 0:
  897.7 67.5 all-reduce.3

commit v2 on v1

--- a/solution.py
+++ b/solution.py
@@ -72,51 +72,64 @@
 GATHER_SEMS = [pltpu.SemaphoreType.DMA((4,))] * 6 + [pltpu.SemaphoreType.DMA((4, 2))] * 2 + [pltpu.SemaphoreType.DMA]
 
 
-def gather_steps(src, dst, rows, sems):
-    zs, zr, xs, xr, ys, yr, ds, dr, own = sems
-    p = places()
-    half = rows // 2
-    blk = lambda b: dst.at[pl.ds(pl.multiple_of(b * rows, rows), rows)]
-    part = lambda b, h: dst.at[pl.ds(pl.multiple_of(b * rows + h * half, half), half)]
-    me, xn, yn = p["me"], p["X"][0], p["Y"][0]
-    mine = pltpu.make_async_copy(src, blk(me), own)
-    mine.start()
-    xc = [push(src, blk(me), xs.at[0], xr.at[0], xn)]
-    yc = [push(src, blk(me), ys.at[0], yr.at[0], yn)]
-    zc = [push(src, blk(me), zs.at[k], zr.at[k], p["col"][k]) for k in (1, 2, 3)]
-    dc = []
-    mine.wait()
-    yield
-    for k in range(4):
+class Gather:
+    def __init__(self, src, dst, rows, sems):
+        self.src, self.dst, self.rows, self.sems, self.p = src, dst, rows, sems, places()
+
+    def block(self, b):
+        return self.dst.at[pl.ds(pl.multiple_of(b * self.rows, self.rows), self.rows)]
+
+    def part(self, b, h):
+        half = self.rows // 2
+        return self.dst.at[pl.ds(pl.multiple_of(b * self.rows + h * half, half), half)]
+
+    def begin(self):
+        zs, zr, xs, xr, ys, yr, _, _, own = self.sems
+        p, src = self.p, self.src
+        me = p["me"]
+        self.mine = pltpu.make_async_copy(src, self.block(me), own)
+        self.mine.start()
+        self.xc = [push(src, self.block(me), xs.at[0], xr.at[0], p["X"][0])]
+        self.yc = [push(src, self.block(me), ys.at[0], yr.at[0], p["Y"][0])]
+        self.zc = [push(src, self.block(me), zs.at[k], zr.at[k], p["col"][k]) for k in (1, 2, 3)]
+        self.dc = []
+
+    def step(self, k):
+        zs, zr, xs, xr, ys, yr, ds, dr, own = self.sems
+        p = self.p
         if k < 3:
-            zc[k].wait_recv()
-            b = p["col"][k + 1]
-            xc.append(push(blk(b), blk(b), xs.at[k + 1], xr.at[k + 1], xn))
-            yc.append(push(blk(b), blk(b), ys.at[k + 1], yr.at[k + 1], yn))
-        xc[k].wait_recv()
-        dc.append(push(part(p["X"][k], 0), part(p["X"][k], 0), ds.at[k, 0], dr.at[k, 0], yn))
-        yc[k].wait_recv()
-        dc.append(push(part(p["Y"][k], 1), part(p["Y"][k], 1), ds.at[k, 1], dr.at[k, 1], xn))
-        yield
-    for c in dc:
-        c.wait_recv()
-    for c in xc + yc + zc + dc:
-        c.wait_send()
+            self.zc[k].wait_recv()
+            b = self.block(p["col"][k + 1])
+            self.xc.append(push(b, b, xs.at[k + 1], xr.at[k + 1], p["X"][0]))
+            self.yc.append(push(b, b, ys.at[k + 1], yr.at[k + 1], p["Y"][0]))
+        b = self.part(p["X"][k], 0)
+        self.xc[k].wait_recv()
+        self.dc.append(push(b, b, ds.at[k, 0], dr.at[k, 0], p["Y"][0]))
+        b = self.part(p["Y"][k], 1)
+        self.yc[k].wait_recv()
+        self.dc.append(push(b, b, ds.at[k, 1], dr.at[k, 1], p["X"][0]))
+
+    def ready(self, k):
+        if k == 0:
+            self.mine.wait()
+        self.dc[2 * k].wait_recv()
+        self.dc[2 * k + 1].wait_recv()
+
+    def end(self):
+        for c in self.xc + self.yc + self.zc + self.dc:
+            c.wait_send()
+
+    def all(self):
+        for k in range(4):
+            self.step(k)
+        for k in range(4):
+            self.ready(k)
+        self.end()
 
 
 def gather_targets():
     p = places()
     return [p["col"][1], p["col"][2], p["col"][3], p["X"][0], p["Y"][0]]
-
-
-def run(*steps):
-    live = list(steps)
-    while live:
-        for s in list(live):
-            try:
-                next(s)
-            except StopIteration:
-                live.remove(s)
 
 
 SCATTER_SEMS = [pltpu.SemaphoreType.DMA((4, 2))] * 2 + [pltpu.SemaphoreType.DMA((4,))] * 6
@@ -131,44 +144,62 @@
     ]
 
 
-def scatter_sum(part, out, rows, bufs, sems):
-    rd, rx, ry, rz = bufs
-    ds, dr, xs, xr, ys, yr, zs, zr = sems
-    p = places()
-    half = rows // 2
-    xn, yn = p["X"][0], p["Y"][0]
-    order = (1, 2, 3, 0)
-    sent = []
-    da, db, xc, yc, zc = {}, {}, {}, {}, {}
-    for k in order:
+class Scatter:
+    def __init__(self, part, out, rows, bufs, sems):
+        self.part, self.out, self.half, self.bufs, self.sems, self.p = part, out, rows // 2, bufs, sems, places()
+        self.da, self.db, self.xc, self.yc, self.zc = {}, {}, {}, {}, {}
+
+    def far(self, k):
+        ds, dr = self.sems[:2]
+        rd, h, p = self.bufs[0], self.half, self.p
         b = p["D"][k]
-        da[k] = push(part.at[b, pl.ds(0, half)], rd.at[2 * k], ds.at[k, 0], dr.at[k, 0], yn)
-        db[k] = push(part.at[b, pl.ds(half, half)], rd.at[2 * k + 1], ds.at[k, 1], dr.at[k, 1], xn)
-    for k in order:
+        self.da[k] = push(self.part.at[b, pl.ds(0, h)], rd.at[2 * k], ds.at[k, 0], dr.at[k, 0], p["Y"][0])
+        self.db[k] = push(self.part.at[b, pl.ds(h, h)], rd.at[2 * k + 1], ds.at[k, 1], dr.at[k, 1], p["X"][0])
+
+    def near(self, k):
+        _, _, xs, xr, ys, yr, _, _ = self.sems
+        rd, rx, ry, _ = self.bufs
+        part, h, p = self.part, self.half, self.p
         b = p["X"][k]
-        da[k].wait_recv()
-        part[b, pl.ds(0, half)] = (part[b, pl.ds(0, half)].astype(F32) + rd[2 * k].astype(F32)).astype(BF)
-        xc[k] = push(part.at[b], rx.at[k], xs.at[k], xr.at[k], xn)
+        self.da[k].wait_recv()
+        part[b, pl.ds(0, h)] = (part[b, pl.ds(0, h)].astype(F32) + rd[2 * k].astype(F32)).astype(BF)
+        self.xc[k] = push(part.at[b], rx.at[k], xs.at[k], xr.at[k], p["X"][0])
         b = p["Y"][k]
-        db[k].wait_recv()
-        part[b, pl.ds(half, half)] = (part[b, pl.ds(half, half)].astype(F32) + rd[2 * k + 1].astype(F32)).astype(BF)
-        yc[k] = push(part.at[b], ry.at[k], ys.at[k], yr.at[k], yn)
-    for k in order:
-        b = p["col"][k]
-        xc[k].wait_recv()
-        yc[k].wait_recv()
+        self.db[k].wait_recv()
+        part[b, pl.ds(h, h)] = (part[b, pl.ds(h, h)].astype(F32) + rd[2 * k + 1].astype(F32)).astype(BF)
+        self.yc[k] = push(part.at[b], ry.at[k], ys.at[k], yr.at[k], p["Y"][0])
+
+    def along(self, k):
+        zs, zr = self.sems[6:]
+        _, rx, ry, rz = self.bufs
+        part = self.part
+        b = self.p["col"][k]
+        self.xc[k].wait_recv()
+        self.yc[k].wait_recv()
         total = part[b].astype(F32) + rx[k].astype(F32) + ry[k].astype(F32)
         if k:
             part[b] = total.astype(BF)
-            zc[k] = push(part.at[b], rz.at[k], zs.at[k], zr.at[k], b)
+            self.zc[k] = push(part.at[b], rz.at[k], zs.at[k], zr.at[k], b)
         else:
-            out[...] = total
-    for k in (1, 2, 3):
-        zc[k].wait_recv()
-        out[...] += rz[k].astype(F32)
-    for group in (da, db, xc, yc, zc):
-        for c in group.values():
-            c.wait_send()
+            self.out[...] = total
+
+    def end(self):
+        for k in (1, 2, 3):
+            self.zc[k].wait_recv()
+            self.out[...] += self.bufs[3][k].astype(F32)
+        for group in (self.da, self.db, self.xc, self.yc, self.zc):
+            for c in group.values():
+                c.wait_send()
+
+    def all(self):
+        order = (1, 2, 3, 0)
+        for k in order:
+            self.far(k)
+        for k in order:
+            self.near(k)
+        for k in order:
+            self.along(k)
+        self.end()
 
 
 ANY = pl.BlockSpec(memory_space=pl.ANY)
@@ -185,8 +216,8 @@
     core = lax.axis_index("grp") % 2
     barrier([lax.rem(me + d, 16) for d in range(1, 16)], pair=True)
     hr = HD // 2
-    g = gather_steps(n_ref, nall, n_ref.shape[0], g_sems)
-    next(g)
+    g = Gather(n_ref, nall, n_ref.shape[0], g_sems)
+    g.begin()
     own = pltpu.make_async_copy(m_ref, mall.at[me], mo)
     own.start()
     mc = []
@@ -212,8 +243,7 @@
         dst = wh.at[pl.ds(pl.multiple_of(s * HD + off, hr), hr)]
         pltpu.make_async_copy(dst, dst, wr.at[s]).wait()
         push_pair(dst, dst, ps.at[s], pr.at[s])
-    for _ in g:
-        pass
+    g.all()
     own.wait()
     for c in mc:
         c.wait()
@@ -254,7 +284,9 @@
 
 def gather_kernel(x_ref, o_ref, *sems):
     barrier(gather_targets())
-    run(gather_steps(x_ref, o_ref, x_ref.shape[0], sems))
+    g = Gather(x_ref, o_ref, x_ref.shape[0], sems)
+    g.begin()
+    g.all()
 
 
 def gather(x, cid):
@@ -276,7 +308,7 @@
     c.start()
     barrier(gather_targets())
     c.wait()
-    scatter_sum(part, o_ref, part.shape[1], bufs, sems)
+    Scatter(part, o_ref, part.shape[1], bufs, sems).all()
 
 
 def scatter(x, cid):
@@ -415,6 +447,137 @@
     )(q, k, v, sq, sk, lse, dc)
 
 
+SLOTS = 80
+COLS = 256
+
+
+def place_of(k, j):
+    me = lax.axis_index("dp")
+    z, y, x = me // 4, (me // 2) % 2, me % 2
+    zk = [z, z + 1 - 2 * (z % 2), (z + 2) % 4, 3 - z][k]
+    jy, jx = j // 2, j % 2
+    return zk * 4 + (y + jy - 2 * y * jy) * 2 + (x + jx - 2 * x * jx)
+
+
+def expert_kernel(
+    n2, cot, pick, pickt, sw, wg_h, wu_h, wd_h,
+    n2g, p1, xr_o, pg_o, hid_o, gg_o, ug_o,
+    nall, call, part, stage, wg, wu, wd, xr, pg, hid, gg, ug, rd, rx, ry, rz, wsem, osem, psem, *sems,
+):
+    rows = n2.shape[0]
+    chunk = 4 * SLOTS
+    loads = [pltpu.make_async_copy(a, b, wsem.at[i]) for i, (a, b) in enumerate([(wg_h, wg), (wu_h, wu), (wd_h, wd)])]
+    for c in loads:
+        c.start()
+    barrier(gather_targets())
+    gn = Gather(n2, nall, rows, sems[:9])
+    gc = Gather(cot, call, rows, sems[9:18])
+    sc = Scatter(part, n2g, rows, (rd, rx, ry, rz), sems[18:])
+    gn.begin()
+    gc.begin()
+    saves = []
+    for k in range(4):
+        gn.step(k)
+        gc.step(k)
+        gn.ready(k)
+        gc.ready(k)
+        for c in saves:
+            c.wait()
+        if k == 0:
+            for c in loads:
+                c.wait()
+
+        def collect(j, carry):
+            b = place_of(k, j)
+            row = pl.ds(pl.multiple_of(b * rows, rows), rows)
+            to = pl.ds(pl.multiple_of(j * SLOTS, SLOTS), SLOTS)
+
+            def cols(n, c):
+                w = pl.ds(pl.multiple_of(n * 512, 512), 512)
+                xr[to, w] = dot(pick[b], nall[row, w], 1, 0).astype(BF)
+                pg[to, w] = (dot(pick[b], call[row, w], 1, 0) * sw[b]).astype(BF)
+                return c
+
+            return lax.fori_loop(0, nall.shape[1] // 512, cols, carry)
+
+        lax.fori_loop(0, 4, collect, 0)
+
+        def inner(n, carry):
+            w = pl.ds(pl.multiple_of(n * COLS, COLS), COLS)
+            gate = dot(xr[...], wg[:, w], 1, 0)
+            up = dot(xr[...], wu[:, w], 1, 0)
+            hg = dot(pg[...], wd[w, :], 1, 1)
+            sig = jax.nn.sigmoid(gate)
+            hid[:, w] = (gate * sig * up).astype(BF)
+            gg[:, w] = (hg * up * sig * (1.0 + gate * (1.0 - sig))).astype(BF)
+            ug[:, w] = (hg * gate * sig).astype(BF)
+            return carry
+
+        lax.fori_loop(0, hid.shape[1] // COLS, inner, 0)
+
+        def outer(n, carry):
+            w = pl.ds(pl.multiple_of(n * COLS, COLS), COLS)
+            eo = dot(hid[...], wd[:, w], 1, 0).astype(BF).astype(F32)
+            rg = (dot(gg[...], wg[w, :], 1, 1) + dot(ug[...], wu[w, :], 1, 1)).astype(BF)
+            for j in range(4):
+                b = place_of(k, j)
+                cut = slice(j * SLOTS, (j + 1) * SLOTS)
+                weighted = (eo[cut] * sw[b]).astype(BF)
+                stage[j, :, w] = dot(pickt[b], weighted, 1, 0).astype(BF)
+                part[b, :, w] = dot(pickt[b], rg[cut], 1, 0).astype(BF)
+            return carry
+
+        lax.fori_loop(0, xr.shape[1] // COLS, outer, 0)
+        sc.far(k)
+        if k >= 1:
+            sc.near(k - 1)
+        if k >= 2:
+            sc.along(k - 2)
+        saves = [
+            pltpu.make_async_copy(a, o.at[k], osem.at[i])
+            for i, (a, o) in enumerate([(xr, xr_o), (pg, pg_o), (hid, hid_o), (gg, gg_o), (ug, ug_o)])
+        ] + [pltpu.make_async_copy(stage.at[j], p1.at[place_of(k, j)], psem.at[j]) for j in range(4)]
+        for c in saves:
+            c.start()
+    gn.end()
+    gc.end()
+    sc.near(3)
+    sc.along(2)
+    sc.along(3)
+    sc.end()
+    for c in saves:
+        c.wait()
+
+
+def expert(n2, cot, pick, pickt, sw, wg, wu, wd, cid):
+    rows, width = n2.shape
+    ff = wg.shape[1]
+    chunk = 4 * SLOTS
+    save = lambda w: jax.ShapeDtypeStruct((4, chunk, w), BF)
+    v = lambda *shape: pltpu.VMEM(shape, BF)
+    return pl.pallas_call(
+        expert_kernel,
+        out_shape=[
+            jax.ShapeDtypeStruct((rows, width), F32),
+            jax.ShapeDtypeStruct((16, rows, width), BF),
+            save(width), save(width), save(ff), save(ff), save(ff),
+        ],
+        in_specs=[ANY, ANY, VM, VM, VM, ANY, ANY, ANY],
+        out_specs=[VM] + [ANY] * 6,
+        scratch_shapes=[
+            v(16 * rows, width), v(16 * rows, width), v(16, rows, width), v(4, rows, width),
+            v(width, ff), v(width, ff), v(ff, width),
+            v(chunk, width), v(chunk, width), v(chunk, ff), v(chunk, ff), v(chunk, ff),
+        ]
+        + scatter_bufs(rows, width)
+        + [pltpu.SemaphoreType.DMA((3,)), pltpu.SemaphoreType.DMA((5,)), pltpu.SemaphoreType.DMA((4,))]
+        + GATHER_SEMS * 2
+        + SCATTER_SEMS,
+        compiler_params=params(cid, 62),
+        name="expert",
+    )(n2, cot, pick, pickt, sw, wg, wu, wd)
+
+
 def rmsnorm(field, gain_row):
     return field * lax.rsqrt(jnp.mean(field * field, -1, keepdims=True) + EPS) * gain_row
 
@@ -445,7 +608,7 @@
     rows, width = tokens.shape
     seq = segments.shape[0]
     me = lax.axis_index("dp")
-    slots = 80
+    slots = SLOTS
     stream = tokens.astype(F32)
     normed = rmsnorm(stream, norm_gain[0]).astype(BF)
     meta = jnp.concatenate([routes.astype(F32).T, route_weight.T], 0)
@@ -463,8 +626,6 @@
     attended = dot(context, dense_out, 1, 1)
     middle = stream + attended
     normed2 = rmsnorm(middle, norm_gain[1]).astype(BF)
-    normed2_all = gather(normed2, 3)
-    cot_all = gather(cotangent, 4)
     mine = meta_all[:, :TOPK] == me.astype(F32)
     member = jnp.sum(mine.astype(F32), 1)
     weight = jnp.sum(jnp.where(mine, meta_all[:, TOPK:], 0.0), 1)
@@ -472,28 +633,17 @@
     before = jnp.cumsum(jnp.sum(member, 1)) - jnp.sum(member, 1)
     kept = (member > 0) & (local + before[:, None] < capacity[0].astype(F32))
     pick = (jnp.arange(slots, dtype=F32)[None, :, None] == local[:, None, :]) & kept[:, None, :]
-    slot_weight = jnp.sum(jnp.where(pick, weight[:, None, :], 0.0), 2).reshape(16 * slots, 1)
+    slot_weight = jnp.sum(jnp.where(pick, weight[:, None, :], 0.0), 2)[:, :, None]
     pick = pick.astype(BF)
-    take = lambda a: jnp.einsum("jst,jtd->jsd", pick, a.reshape(16, rows, width), preferred_element_type=F32).reshape(16 * slots, width)
-    put = lambda a: jnp.einsum("jst,jsd->jtd", pick, a.reshape(16, slots, width), preferred_element_type=F32).reshape(seq, width).astype(BF)
-    xr = take(normed2_all).astype(BF)
-    pg = (take(cot_all) * slot_weight).astype(BF)
-    gate = dot(xr, gate_weight[0], 1, 0)
-    up = dot(xr, up_weight[0], 1, 0)
-    sig = jax.nn.sigmoid(gate)
-    hidden = (gate * sig * up).astype(BF)
-    eo = dot(hidden, down_weight[0], 1, 0).astype(BF)
-    mix_part = put((eo.astype(F32) * slot_weight).astype(BF))
-    hg = dot(pg, down_weight[0], 1, 1)
-    gg = (hg * up * sig * (1.0 + gate * (1.0 - sig))).astype(BF)
-    ug = (hg * gate * sig).astype(BF)
-    rg = (dot(gg, gate_weight[0], 1, 1) + dot(ug, up_weight[0], 1, 1)).astype(BF)
-    back_part = put(rg)
+    n2g, mix_part, xr, pg, hidden, gg, ug = expert(
+        normed2, cotangent, pick, pick.transpose(0, 2, 1), slot_weight, gate_weight[0], up_weight[0], down_weight[0], 3
+    )
+    flat = lambda a: a.reshape(-1, a.shape[2])
+    xr, pg, hidden, gg, ug = [flat(a) for a in (xr, pg, hidden, gg, ug)]
     down_g = dot(hidden, pg, 0, 0)
     gate_g = dot(xr, gg, 0, 0)
     up_g = dot(xr, ug, 0, 0)
-    mixture = scatter(mix_part, 5)
-    n2g = scatter(back_part, 6)
+    mixture = scatter(mix_part.reshape(seq, width), 5)
     layer = middle + mixture
     own_seg = lax.dynamic_slice_in_dim(segments, me * rows, rows)
     valid = (own_seg != 0).astype(F32)

time: 1160 us -> 1110 us (0.957)
  matrix products: 148 us -> 66.1 us
  Pallas kernels: 830 us -> 872 us
    pallas_call x0 -> x1, Pallas kernels: none -> 310 us  [expert(): pl.pallas_call(expert_kernel, out_shape=[jax.ShapeDtypeStruct((rows, widt...]
    pallas_call x3 -> x1, Pallas kernels: 252 us -> 85.4 us  [gather(): pl.pallas_call(gather_kernel, out_shape=jax.ShapeDtypeStruct((16 * rows,...]
    pallas_call x4 -> x3, Pallas kernels: 361 us -> 262 us  [scatter(): pl.pallas_call(scatter_kernel, out_shape=jax.ShapeDtypeStruct((rows, widt...]
    dot_general x15 -> x9, matrix products: 121 us -> 66.1 us  [dot(): lax.dot_general(a, b, (((ca,), (cb,)), ((), ())), preferred_element_type=...]
    dot_general x4 -> x0, matrix products: 27.3 us -> none  [the longest x2 15.8 us: per_device(): jnp.einsum('jst,jtd->jsd', pick, a.reshape(16, rows, width), preferred_el...]
  transfers between devices with their start and end apart: 1 -> 1, of which waited for: 0 -> 0; matrix products, arithmetic and copies ran while one was open for 1% -> 2% of each run, Pallas kernels for 9% -> 9%
where the time goes in v2:
time: 1110 us; the launch traced here: 1100 us
  Pallas kernels  872 us (79%)
  blocking collectives  79.5 us (7%)
  matrix products  66.1 us (6%)
  other arithmetic  53.7 us (5%)
  local copies, waits for them, and re-layouts  17.5 us (2%)
  between operations  16.1 us (1%)
    pallas_call x1, Pallas kernels, expert(): pl.pallas_call(expert_kernel, out_shape=[jax.ShapeDtypeStruct((rows, widt...  310 us
    pallas_call x3, Pallas kernels, scatter(): pl.pallas_call(scatter_kernel, out_shape=jax.ShapeDtypeStruct((rows, widt...  262 us
    pallas_call x1, Pallas kernels, front(): pl.pallas_call(front_kernel, out_shape=[jax.ShapeDtypeStruct((16 * rows,...  127 us
    pallas_call x1, Pallas kernels, gather(): pl.pallas_call(gather_kernel, out_shape=jax.ShapeDtypeStruct((16 * rows,...  85.4 us
    dot_general x9, matrix products, dot(): lax.dot_general(a, b, (((ca,), (cb,)), ((), ())), preferred_element_type=...  66.1 us
    psum x1, blocking collectives, per_device(): seq_sums, gain_dp = lax.psum((sums, jnp.stack([gain1, gain2])), 'dp')  63 us
    pallas_call x2, Pallas kernels, swap(): pl.pallas_call(swap_kernel, out_shape=jax.ShapeDtypeStruct(x.shape, x.dty...  33 us
    pallas_call x1, Pallas kernels, give_back(): pl.pallas_call(return_kernel, out_shape=jax.ShapeDtypeStruct(x.shape, x.d...  29.3 us
  transfers between devices with their start and end apart: 1, of which 0 were waited for; matrix products, arithmetic and copies ran while one was open for 2% of the time, Pallas kernels for 9%

profile of v2, /device:TPU:5, one launch (start us, length us, event | category | flops | bytes accessed | tf_op | source)
XLA Modules:
  0.0 1104.6 jit_solution(8769390630605660709)
XLA Ops:
  7.9 1.2 fusion.42
  9.2 0.7 convert_bitcast_fusion
  9.8 0.8 fusion.53
  10.7 1.3 pad_maximum_fusion.3.m_ref
  11.9 2.0 fusion.22.n_ref
  14.0 126.9 %front.1 = (bf16[2048,2048]{1,0:T(8,128)(2,1)}, f32[16,16,128]{2,1,0:T(8,128)}, bf16[384,2048]{1,0:T(8,128)(2,1)}) custom-call(bf16[128,2048]{1,0:T(8,128)(2,1)} %fusion.22.n_ref, f32[16,128]{1,0:T(8,128)} %pad_maximum_fusion.3.m_ref, bf16[384,2048]{1,0:T(8,128)(2,1)} %w_ref.1), custom_call_target="tpu_custom_call" | custom-call | tf_op jit(solution)/shard_map/front/pallas_call | solution.py:267
  140.9 1.1 select_reduce_fusion.1
  142.6 0.9 fusion.47.pick
  143.4 1.4 fusion.45.pickt
  144.8 0.4 copy.55.sq
  145.2 85.4 %gather_2.1 = bf16[2048,2048]{1,0:T(8,128)(2,1)} custom-call(bf16[128,2048]{1,0:T(8,128)(2,1)} %x_ref.1), custom_call_target="tpu_custom_call" | custom-call | tf_op jit(solution)/shard_map/gather_2/pallas_call | solution.py:294
  230.6 0.4 select_reduce_fusion
  230.9 1.1 copy.58.sw
  232.0 6.9 fusion.54
  239.0 5.1 fusion.37
  244.1 0.6 pad_maximum_fusion
  244.7 10.6 attend.1
  255.4 1.0 copy-done.9
  256.3 0.8 copy-done.10
  257.1 10.9 swap_1.1
  268.1 1.3 copy.56
  269.4 6.6 multiply_reduce_fusion.5
  276.1 1.0 multiply_convert_fusion.n2
  277.0 309.9 %expert.1 = (f32[128,2048]{1,0:T(8,128)}, bf16[16,128,2048]{2,1,0:T(8,128)(2,1)}, bf16[4,320,2048]{2,1,0:T(8,128)(2,1)}, bf16[4,320,2048]{2,1,0:T(8,128)(2,1)}, ...) custom-call(bf16[128,2048]{1,0:T(8,128)(2,1)} %multiply_convert_fusion.n2, ...), custom_call_target="tpu_custom_call" | custom-call | tf_op jit(solution)/shard_map/expert/pallas_call | solution.py:558
  586.9 79.9 %scatter_5.1 = f32[128,2048]{1,0:T(8,128)} custom-call(bf16[16,128,2048]{2,1,0:T(8,128)(2,1)} %get-tuple-element.28.p_ref), custom_call_target="tpu_custom_call" | custom-call | tf_op jit(solution)/shard_map/scatter_5/pallas_call | solution.py:316
  666.8 2.3 multiply_reduce_fusion.2
  669.1 0.3 fusion.40
  669.5 5.1 convolution_convert_fusion.3
  674.6 5.8 convolution_convert_fusion.1
  680.7 1.1 copy.60
  681.7 22.0 %swap_7.1 = bf16[16,128,128]{2,1,0:T(8,128)(2,1)} custom-call(bf16[16,128,128]{2,1,0:T(8,128)(2,1)} %bitcast.85), custom_call_target="tpu_custom_call" | custom-call | tf_op jit(solution)/shard_map/swap_7/pallas_call | solution.py:344
  703.8 1.0 copy-done.5
  704.9 14.8 %attend_back.1 = (f32[2048,128]{1,0:T(8,128)S(1)}, f32[128,2048]{1,0:T(8,128)S(1)}, f32[128,2048]{1,0:T(8,128)S(1)}) custom-call(bf16[2048,128]{1,0:T(8,128)(2,1)S(1)} %copy-done.2, bf16[2048,128]{1,0:T(8,128)(2,1)S(1)} %copy-done.4, bf16[2048,128]{1,0:T(8,128)(2,1)S(1)} %slice.96.v, s32[2048,1]{1,0:T(8,128)} %copy-done, s32[1,2048]{1,0:T(1,128)S(1)} %bitcast.74, ...), custom_call_target="tpu_custom_call" | custom-call | tf_op jit(solution)/shard_map/attend_back/pallas_call | solution.py:439
  719.7 1.0 copy-done.6
  720.6 1.0 copy-done.8
  721.6 1.5 copy.62
  723.2 5.8 fusion.31
  729.0 1.3 copy.66
  730.3 1.2 copy.65
  731.5 1.2 copy.63
  733.2 9.1 convolution_convert_fusion.2
  742.4 7.2 fusion
  749.6 7.2 fusion.1
  756.8 85.0 %scatter_10.1 = f32[128,2048]{1,0:T(8,128)} custom-call(bf16[16,128,2048]{2,1,0:T(8,128)(2,1)} %bitcast.75), custom_call_target="tpu_custom_call" | custom-call | tf_op jit(solution)/shard_map/scatter_10/pallas_call | solution.py:316
  841.8 2.1 convert_element_type.182
  843.9 9.7 fusion.2
  853.6 1.4 copy-done.23
  855.0 8.4 convolution_convert_fusion
  863.4 97.1 %scatter_9.1 = f32[128,2048]{1,0:T(8,128)} custom-call(bf16[16,128,2048]{2,1,0:T(8,128)(2,1)} %bitcast.77), custom_call_target="tpu_custom_call" | custom-call | tf_op jit(solution)/shard_map/scatter_9/pallas_call | solution.py:316
  960.5 0.7 select_reduce_fusion.4
  961.8 2.0 pad_maximum_fusion.4
  963.9 1.6 fusion.23
  965.5 63.0 %all-reduce = (bf16[2,2048]{1,0:T(2,128)(2,1)S(1)}, f32[4]{0:T(128)S(1)}) all-reduce(f32[2,2048]{1,0:T(2,128)S(1)} %pad_maximum_fusion.2, f32[4]{0:T(128)S(1)} %pad_maximum_fusion.4), channel_id=1, replica_groups=mesh['grp'=2,'dp'=16] {'dp'}, use_global_device_ids=true, to_apply=%region_17.18 | all-reduce | flops 4100 | bytes 24608 | tf_op jit(solution)/shard_map/psum | solution.py:675
  1028.5 0.6 slice.68
  1029.1 16.5 %psum.62 = bf16[2,2048]{1,0:T(2,128)(2,1)S(1)} all-reduce(bf16[2,2048]{1,0:T(2,128)(2,1)S(1)} %get-tuple-element.54), channel_id=1, replica_groups=mesh['grp'=2,'dp'=16] {'grp'}, use_global_device_ids=true, to_apply=%region_18.19 | all-reduce | flops 4096 | bytes 16384 | tf_op jit(solution)/shard_map/psum | solution.py:677
  1045.6 0.6 convert_element_type.188
  1046.2 1.2 sqrt_bitcast_fusion
  1047.4 2.5 fusion.41
  1049.9 29.3 %give_back.1 = bf16[3,128,2048]{2,1,0:T(8,128)(2,1)} custom-call(bf16[3,128,2048]{2,1,0:T(8,128)(2,1)} %get-tuple-element.56.x_ref), custom_call_target="tpu_custom_call" | custom-call | tf_op jit(solution)/shard_map/give_back/pallas_call | solution.py:379
  1079.2 1.1 convert_element_type.183
  1080.3 4.0 bitcast_convert_fusion.3
  1084.3 4.4 broadcast_in_dim.74
  1088.7 4.4 broadcast_in_dim.76
  1093.2 4.4 broadcast_in_dim.78
  (82 shorter events, 1.5 us)
Async XLA Ops:
  7.2 137.6 %copy-start.24 = (s32[2048]{0:T(1024)S(1)}, s32[2048]{0:T(1024)}, u32[]{:S(2)}) copy-start(s32[2048]{0:T(1024)} %param.13) | copy-start | bytes 24580
  7.2 1042.7 %all-reduce.4.cloned.1.call-start = ((), (), s32[]{:S(2)}) async-start(), calls=%async_computation | async-start | bytes 29360128 | tf_op jit(solution)/shard_map/psum | solution.py:669
  145.2 99.5 %copy-start = (s32[2048,1]{1,0:T(8,128)}, s32[2048,1]{1,0:T(8,128)S(1)}, u32[]{:S(2)}) copy-start(s32[2048,1]{1,0:T(8,128)S(1)} %copy.55.sq) | copy-start | bytes 24580
  145.2 86.9 %copy-start.28 = (bf16[384,2048]{1,0:T(8,128)(2,1)S(1)}, bf16[384,2048]{1,0:T(8,128)(2,1)}, u32[]{:S(2)}) copy-start(bf16[384,2048]{1,0:T(8,128)(2,1)} %get-tuple-element.25) | copy-start | bytes 4718596
  244.7 10.7 copy-start.1
  244.7 12.4 %copy-start.3 = (bf16[2048,128]{1,0:T(8,128)(2,1)}, bf16[2048,128]{1,0:T(8,128)(2,1)S(1)}, u32[]{:S(2)}) copy-start(bf16[2048,128]{1,0:T(8,128)(2,1)S(1)} %get-tuple-element.80.k) | copy-start | bytes 1572868
  255.4 1.0 copy-start.9
  256.3 0.8 copy-start.10
  269.4 6.7 copy-start.14
  586.9 79.9 %copy-start.19 = (f32[128,2048]{1,0:T(8,128)S(1)}, f32[128,2048]{1,0:T(8,128)}, u32[]{:S(2)}) copy-start(f32[128,2048]{1,0:T(8,128)} %get-tuple-element.29) | copy-start | bytes 3145732
  666.8 2.3 copy-start.20
  669.5 5.1 copy-start.11
  669.5 5.1 copy-start.15
  680.4 23.4 %copy-start.2 = (bf16[2048,128]{1,0:T(8,128)(2,1)S(1)}, bf16[2048,128]{1,0:T(8,128)(2,1)}, u32[]{:S(2)}) copy-start(bf16[2048,128]{1,0:T(8,128)(2,1)} %copy-done.1) | copy-start | bytes 1572868
  680.4 23.4 %copy-start.4 = (bf16[2048,128]{1,0:T(8,128)(2,1)S(1)}, bf16[2048,128]{1,0:T(8,128)(2,1)}, u32[]{:S(2)}) copy-start(bf16[2048,128]{1,0:T(8,128)(2,1)} %copy-done.3) | copy-start | bytes 1572868
  703.8 1.0 copy-start.5
  719.7 1.0 copy-start.6
  720.6 1.0 copy-start.8
  728.9 4.1 copy-start.7
  733.1 9.3 slice-start
  733.1 9.2 copy-start.22
  733.2 9.2 slice-start.1
  733.2 9.2 copy-start.27
  742.4 7.2 copy-start.26
  756.8 87.1 %copy-start.25 = (bf16[4,320,1024]{2,1,0:T(8,128)(2,1)S(1)}, bf16[4,320,1024]{2,1,0:T(8,128)(2,1)}, u32[]{:S(2)}) copy-start(bf16[4,320,1024]{2,1,0:T(8,128)(2,1)} %get-tuple-element.37) | copy-start | bytes 7864324
  853.6 1.4 copy-start.23
  863.4 100.5 %copy-start.13 = (bf16[128,2048]{1,0:T(8,128)(2,1)S(1)}, bf16[128,2048]{1,0:T(8,128)(2,1)}, u32[]{:S(2)}) copy-start(bf16[128,2048]{1,0:T(8,128)(2,1)} %param.12) | copy-start | bytes 1572868
  863.4 184.0 %copy-start.12 = (f32[128,2048]{1,0:T(8,128)S(1)}, f32[128,2048]{1,0:T(8,128)}, u32[]{:S(2)}) copy-start(f32[128,2048]{1,0:T(8,128)} %copy-done.11) | copy-start | bytes 3145732
  1049.9 29.3 %copy-start.21 = (bf16[128,2048]{1,0:T(8,128)(2,1)S(1)}, bf16[128,2048]{1,0:T(8,128)(2,1)}, u32[]{:S(2)}) copy-start(bf16[128,2048]{1,0:T(8,128)(2,1)} %get-tuple-element.57) | copy-start | bytes 1572868
  1079.2 5.1 copy-start.18
  1084.3 4.4 copy-start.17
  1088.7 4.4 copy-start.16
Sparse Core Ops, SparseCore 0:
  853.8 67.4 all-reduce.3

commit v3 on v2

--- a/solution.py
+++ b/solution.py
@@ -302,30 +302,6 @@
     )(x)
 
 
-def scatter_kernel(p_ref, o_ref, part, load, *rest):
-    bufs, sems = rest[:4], rest[4:]
-    c = pltpu.make_async_copy(p_ref, part, load)
-    c.start()
-    barrier(gather_targets())
-    c.wait()
-    Scatter(part, o_ref, part.shape[1], bufs, sems).all()
-
-
-def scatter(x, cid):
-    rows, width = x.shape[0] // 16, x.shape[1]
-    return pl.pallas_call(
-        scatter_kernel,
-        out_shape=jax.ShapeDtypeStruct((rows, width), F32),
-        in_specs=[ANY],
-        out_specs=VM,
-        scratch_shapes=[pltpu.VMEM((16, rows, width), BF), pltpu.SemaphoreType.DMA]
-        + scatter_bufs(rows, width)
-        + SCATTER_SEMS,
-        compiler_params=params(cid),
-        name=f"scatter_{cid}",
-    )(x.reshape(16, rows, width))
-
-
 def swap_kernel(x_ref, o_ref, ss, rs, lo):
     me = lax.axis_index("dp")
     barrier([lax.rem(me + d, 16) for d in range(1, 16)])
@@ -349,41 +325,6 @@
         scratch_shapes=[pltpu.SemaphoreType.DMA((16,))] * 2 + [pltpu.SemaphoreType.DMA],
         compiler_params=params(cid),
         name=f"swap_{cid}",
-    )(x)
-
-
-def return_kernel(x_ref, o_ref, ss, rs):
-    me = lax.axis_index("dp")
-    barrier([lax.rem(me + d, 16) for d in range(1, 16)])
-    for s in range(3):
-        b = 16 * s + me
-        to, slot = b // 3, lax.rem(b, 3)
-
-        @pl.when(to != me)
-        def _():
-            push(x_ref.at[s], o_ref.at[slot], ss.at[s], rs.at[slot], to)
-
-        @pl.when(to == me)
-        def _():
-            pltpu.make_async_copy(x_ref.at[s], o_ref.at[slot], rs.at[slot]).start()
-
-    for s in range(3):
-        pltpu.make_async_copy(x_ref.at[s], o_ref.at[s], rs.at[s]).wait()
-
-        @pl.when((16 * s + me) // 3 != me)
-        def _():
-            pltpu.make_async_copy(x_ref.at[s], o_ref.at[s], ss.at[s]).wait()
-
-
-def give_back(x, cid):
-    return pl.pallas_call(
-        return_kernel,
-        out_shape=jax.ShapeDtypeStruct(x.shape, x.dtype),
-        in_specs=[ANY],
-        out_specs=ANY,
-        scratch_shapes=[pltpu.SemaphoreType.DMA((3,))] * 2,
-        compiler_params=params(cid),
-        name="give_back",
     )(x)
 
 
@@ -414,37 +355,6 @@
         compiler_params=pltpu.CompilerParams(vmem_limit_bytes=48 * MIB),
         name="attend",
     )(q, k, v, sq, sk)
-
-
-def attend_back_kernel(q, k, v, sq, sk, lse, dc, dq, dkt, dvt):
-    @pl.when(pl.program_id(0) == 0)
-    def _():
-        dkt[...] = jnp.zeros_like(dkt)
-        dvt[...] = jnp.zeros_like(dvt)
-
-    s = lax.dot_general(q[...], k[...], (((1,), (1,)), ((), ())), preferred_element_type=F32)
-    prob = jnp.where(sq[...] == sk[...], jnp.exp2(s * (SCALE * LOG2E) - lse[...]), 0.0)
-    dp = lax.dot_general(dc[...], v[...], (((1,), (1,)), ((), ())), preferred_element_type=F32)
-    delta = jnp.sum(prob * dp, -1, keepdims=True)
-    ds = (prob * (dp - delta)).astype(BF)
-    dq[...] = jnp.dot(ds, k[...], preferred_element_type=F32) * SCALE
-    dkt[...] += lax.dot_general(q[...], ds, (((0,), (0,)), ((), ())), preferred_element_type=F32) * SCALE
-    dvt[...] += lax.dot_general(dc[...], prob.astype(BF), (((0,), (0,)), ((), ())), preferred_element_type=F32)
-
-
-def attend_back(q, k, v, sq, sk, lse, dc):
-    n = q.shape[0]
-    row = lambda w: pl.BlockSpec((QB, w), lambda i: (i, 0))
-    full = lambda r, w: pl.BlockSpec((r, w), lambda i: (0, 0))
-    return pl.pallas_call(
-        attend_back_kernel,
-        grid=(n // QB,),
-        out_shape=[jax.ShapeDtypeStruct((n, HD), F32), jax.ShapeDtypeStruct((HD, n), F32), jax.ShapeDtypeStruct((HD, n), F32)],
-        in_specs=[row(HD), full(n, HD), full(n, HD), row(1), full(1, n), row(1), row(HD)],
-        out_specs=[row(HD), full(HD, n), full(HD, n)],
-        compiler_params=pltpu.CompilerParams(vmem_limit_bytes=48 * MIB),
-        name="attend_back",
-    )(q, k, v, sq, sk, lse, dc)
 
 
 SLOTS = 80
@@ -578,23 +488,314 @@
     )(n2, cot, pick, pickt, sw, wg, wu, wd)
 
 
+TILE = (256, 1024)
+
+
+def weights_kernel(
+    p1, xr_h, pg_h, hid_h, gg_h, ug_h,
+    mix, gate_o, up_o, down_o,
+    part, xr, pg, hid, gg, ug, own, give, got, rd, rx, ry, rz, load, lsem, gs, gr, os_, *sems,
+):
+    loads = [
+        pltpu.make_async_copy(a, b, lsem.at[i])
+        for i, (a, b) in enumerate([(p1, part), (xr_h, xr), (gg_h, gg), (ug_h, ug), (hid_h, hid), (pg_h, pg)])
+    ]
+    for c in loads:
+        c.start()
+    barrier(gather_targets(), pair=True)
+    sc = Scatter(part, mix, part.shape[1], (rd, rx, ry, rz), sems)
+    loads[0].wait()
+    order = (1, 2, 3, 0)
+    for k in order:
+        sc.far(k)
+    for c in loads[1:]:
+        c.wait()
+    r, w = TILE
+
+    def product(m, t):
+        if m < 2:
+            return dot(xr[:, pl.ds(pl.multiple_of(t * r, r), r)], (gg, ug)[m][...], 0, 0)
+        i, j = t // 2, t % 2
+        return dot(hid[:, pl.ds(pl.multiple_of(i * r, r), r)], pg[:, pl.ds(pl.multiple_of(j * w, w), w)], 0, 0)
+
+    def home(m, t):
+        if m < 2:
+            return (gate_o, up_o)[m].at[pl.ds(pl.multiple_of(t * r, r), r)]
+        i, j = t // 2, t % 2
+        return down_o.at[pl.ds(pl.multiple_of(i * r, r), r), pl.ds(pl.multiple_of(j * w, w), w)]
+
+    for m in range(3):
+
+        def sent(t, m=m):
+            s = lax.rem(t, 2)
+            return pltpu.make_async_remote_copy(
+                src_ref=give.at[s], dst_ref=got.at[m, t], send_sem=gs.at[s], recv_sem=gr.at[m, t],
+                device_id={"grp": partner()}, device_id_type=MESH,
+            )
+
+        def saved(t, m=m):
+            s = lax.rem(t, 2)
+            return pltpu.make_async_copy(own.at[s], home(m, t), os_.at[s])
+
+        def finish(t, m=m):
+            s = lax.rem(t, 2)
+            sent(t, m).wait_recv()
+            own[s] = own[s] + got[m, t].astype(F32)
+            saved(t, m).start()
+
+        def body(t, carry, m=m):
+            s = lax.rem(t, 2)
+
+            @pl.when(t >= 2)
+            def _():
+                sent(t - 2, m).wait_send()
+                saved(t - 2, m).wait()
+
+            low = product(m, t).astype(BF)
+            give[s] = low
+            own[s] = low.astype(F32)
+            sent(t, m).start()
+
+            @pl.when(t >= 1)
+            def _():
+                finish(t - 1, m)
+
+            return carry
+
+        lax.fori_loop(0, 8, body, 0)
+        finish(7, m)
+        for t in (6, 7):
+            sent(t, m).wait_send()
+            saved(t, m).wait()
+        if m == 0:
+            for k in order:
+                sc.near(k)
+        if m == 1:
+            sc.along(1)
+            sc.along(2)
+    sc.along(3)
+    sc.along(0)
+    sc.end()
+
+
+def expert_weights(p1, xr, pg, hid, gg, ug, cid):
+    _, rows, width = p1.shape
+    n, ff = gg.shape
+    r, w = TILE
+    v = lambda *shape: pltpu.VMEM(shape, BF)
+    return pl.pallas_call(
+        weights_kernel,
+        out_shape=[
+            jax.ShapeDtypeStruct((rows, width), F32),
+            jax.ShapeDtypeStruct((width, ff), F32),
+            jax.ShapeDtypeStruct((width, ff), F32),
+            jax.ShapeDtypeStruct((ff, width), F32),
+        ],
+        in_specs=[ANY] * 6,
+        out_specs=[VM] + [ANY] * 3,
+        scratch_shapes=[
+            v(16, rows, width), v(n, width), v(n, width), v(n, ff), v(n, ff), v(n, ff),
+            pltpu.VMEM((2, r, w), F32), v(2, r, w), v(3, 8, r, w),
+        ]
+        + scatter_bufs(rows, width)
+        + [pltpu.SemaphoreType.DMA, pltpu.SemaphoreType.DMA((6,)), pltpu.SemaphoreType.DMA((2,))]
+        + [pltpu.SemaphoreType.DMA((3, 8)), pltpu.SemaphoreType.DMA((2,))]
+        + SCATTER_SEMS,
+        compiler_params=params(cid, 62),
+        name="expert_weights",
+    )(p1, xr, pg, hid, gg, ug)
+
+
+def back_kernel(
+    cg, q, k, v, sq, sk, lse, cosf, sinf, wh, nall, ag, ctx,
+    ngrad, out_t, qkv_t,
+    cgh, dkt, dvt, pgrad, pgt, opart, opair, osum, ostage, ord_, orx, ory, orz,
+    part, rd, rx, ry, rz, ntile, qpart, qpair,
+    ss, rs, lo, ops, opr, ofs, ofr, nsem, qs, qr, ts, tr, fs, fr, *sems,
+):
+    me = lax.axis_index("dp")
+    core = lax.axis_index("grp") % 2
+    hr = HD // 2
+    mine, other = pl.multiple_of(core * hr, hr), pl.multiple_of((1 - core) * hr, hr)
+    blk = lambda b: pl.ds(pl.multiple_of(b * HD, HD), HD)
+    barrier([lax.rem(me + d, 16) for d in range(1, 16)], pair=True)
+    hop = lambda d: pltpu.make_async_remote_copy(
+        src_ref=cg.at[:, blk(lax.rem(me + d, 16))], dst_ref=cgh.at[blk(me)], send_sem=ss.at[d], recv_sem=rs.at[d],
+        device_id={"dp": lax.rem(me + d, 16)}, device_id_type=MESH,
+    )
+    stay = pltpu.make_async_copy(cg.at[:, blk(me)], cgh.at[blk(me)], lo)
+    stay.start()
+    for d in range(1, 16):
+        hop(d).start()
+    tiles = [
+        pltpu.make_async_copy(nall.at[:, pl.ds(t * 256, 256)], ntile.at[t % 2], nsem.at[t % 2])
+        for t in range(wh.shape[1] // 256)
+    ]
+
+    def out_block(b, carry):
+        opart[b] = dot(ag[:, blk(b)], ctx[...], 0, 0).astype(BF)
+        return carry
+
+    lax.fori_loop(0, 16, out_block, 0)
+    pair = push_pair(opart.at[:, pl.ds(other, hr)], opair, ops, opr)
+    dkt[...] = jnp.zeros_like(dkt)
+    dvt[...] = jnp.zeros_like(dvt)
+    so = Scatter(opair, osum, hr, (ord_, orx, ory, orz), sems[:8])
+    sn = Scatter(part, ngrad, HD, (rd, rx, ry, rz), sems[8:16])
+    pair.wait_recv()
+
+    def out_pair(b, carry):
+        opair[b] = (opair[b].astype(F32) + opart[b, pl.ds(mine, hr)].astype(F32)).astype(BF)
+        return carry
+
+    lax.fori_loop(0, 16, out_pair, 0)
+    stay.wait()
+    for d in range(1, 16):
+        hop(d).wait_recv()
+    order = (1, 2, 3, 0)
+    for j in order:
+        so.far(j)
+
+    def attend_rows(i, carry):
+        row = blk(i)
+        s = dot(q[row], k[...], 1, 1)
+        prob = jnp.where(sq[row] == sk[...], jnp.exp2(s * (SCALE * LOG2E) - lse[row]), 0.0)
+        dp = dot(cgh[row], v[...], 1, 1)
+        delta = jnp.sum(prob * dp, -1, keepdims=True)
+        ds = (prob * (dp - delta)).astype(BF)
+        dq = dot(ds, k[...], 1, 0) * SCALE
+        dq = dq * cosf[row] - pltpu.roll(dq, HD // 2, 1) * sinf[row]
+        pgrad[row, :HD] = dq.astype(BF)
+        pgt[:HD, row] = dq.T.astype(BF)
+        dkt[...] += dot(q[row], ds, 0, 0)
+        dvt[...] += dot(cgh[row], prob.astype(BF), 0, 0)
+        return carry
+
+    n = q.shape[0] // HD
+    lax.fori_loop(0, n // 2, attend_rows, 0)
+    for j in order:
+        so.near(j)
+    lax.fori_loop(n // 2, n, attend_rows, 0)
+    for j in order:
+        so.along(j)
+
+    def turn_back(i, carry):
+        row = blk(i)
+        dk = dkt[:, row].T * SCALE
+        dk = dk * cosf[row] - pltpu.roll(dk, HD // 2, 1) * sinf[row]
+        pgrad[row, HD : 2 * HD] = dk.astype(BF)
+        pgt[HD : 2 * HD, row] = dk.T.astype(BF)
+        dv = dvt[:, row]
+        pgrad[row, 2 * HD :] = dv.T.astype(BF)
+        pgt[2 * HD :, row] = dv.astype(BF)
+        return carry
+
+    lax.fori_loop(0, n, turn_back, 0)
+    tiles[0].start()
+
+    def back_block(j, kk):
+        b = place_of(kk, j)
+        part[b] = dot(pgrad[blk(b)], wh[...], 1, 0).astype(BF)
+
+    for kk in order:
+        back_block(3, kk)
+        sn.far(kk)
+    for t, c in enumerate(tiles):
+        if t + 1 < len(tiles):
+            tiles[t + 1].start()
+        c.wait()
+        qpart[:, t * 256 : (t + 1) * 256] = dot(pgt[...], ntile[t % 2], 1, 0).astype(BF)
+    qc = [push_pair(qpart.at[pl.ds(s * HD + other, hr)], qpair.at[s], qs.at[s], qr.at[s]) for s in range(3)]
+    so.end()
+    ostage[...] = osum[...].astype(BF)
+    keep = pltpu.make_async_copy(ostage, out_t.at[pl.ds(mine, hr)], lo)
+    keep.start()
+    give = push_pair(ostage, out_t.at[pl.ds(mine, hr)], ofs, ofr)
+    for kk in order:
+        back_block(1, kk)
+        back_block(2, kk)
+        sn.near(kk)
+    for s in range(3):
+        qc[s].wait_recv()
+        qpair[s] = (qpair[s].astype(F32) + qpart[pl.ds(s * HD + mine, hr)].astype(F32)).astype(BF)
+        b = 16 * s + me
+        to, slot = b // 3, lax.rem(b, 3)
+        dst = qkv_t.at[pl.ds(pl.multiple_of(slot * HD + core * hr, hr), hr)]
+
+        @pl.when(to != me)
+        def _():
+            push(qpair.at[s], dst, ts.at[s], tr.at[slot], to)
+
+        @pl.when(to == me)
+        def _():
+            pltpu.make_async_copy(qpair.at[s], dst, tr.at[slot]).start()
+
+    for kk in order:
+        back_block(0, kk)
+    for kk in order:
+        sn.along(kk)
+    fc = []
+    for s in range(3):
+        here = qkv_t.at[pl.ds(pl.multiple_of(s * HD + core * hr, hr), hr)]
+        pltpu.make_async_copy(here, here, tr.at[s]).wait()
+        fc.append(push_pair(here, here, fs.at[s], fr.at[s]))
+    sn.end()
+    for s in range(3):
+
+        @pl.when((16 * s + me) // 3 != me)
+        def _():
+            pltpu.make_async_copy(qpair.at[s], qpair.at[s], ts.at[s]).wait()
+
+    keep.wait()
+    give.wait()
+    pair.wait_send()
+    for c in qc:
+        c.wait_send()
+    for c in fc:
+        c.wait()
+    for d in range(1, 16):
+        hop(d).wait_send()
+
+
+def back(cg, q, k, v, sq, sk, lse, cosf, sinf, wh, nall, ag, ctx, cid):
+    rows, width = cg.shape
+    seq = q.shape[0]
+    vb = lambda *shape: pltpu.VMEM(shape, BF)
+    vf = lambda *shape: pltpu.VMEM(shape, F32)
+    sem = lambda *shape: pltpu.SemaphoreType.DMA(shape) if shape else pltpu.SemaphoreType.DMA
+    return pl.pallas_call(
+        back_kernel,
+        out_shape=[
+            jax.ShapeDtypeStruct((rows, width), F32),
+            jax.ShapeDtypeStruct((rows, width), BF),
+            jax.ShapeDtypeStruct((3 * HD, width), BF),
+        ],
+        in_specs=[ANY] + [VM] * 9 + [ANY, VM, VM],
+        out_specs=[VM, ANY, ANY],
+        scratch_shapes=[
+            vb(seq, HD), vf(HD, seq), vf(HD, seq), vb(seq, 3 * HD), vb(3 * HD, seq),
+            vb(16, rows, width), vb(16, rows // 2, width), vf(rows // 2, width), vb(rows // 2, width),
+        ]
+        + scatter_bufs(rows // 2, width)
+        + [vb(16, rows, width)]
+        + scatter_bufs(rows, width)
+        + [vb(2, seq, 256), vb(3 * HD, width), vb(3, HD // 2, width)]
+        + [sem(16), sem(16), sem(), sem(), sem(), sem(), sem(), sem(2), sem(3), sem(3), sem(3), sem(3), sem(3), sem(3)]
+        + SCATTER_SEMS * 2,
+        compiler_params=params(cid, 62),
+        name="back",
+    )(cg, q, k, v, sq, sk, lse, cosf, sinf, wh, nall, ag, ctx)
+
+
 def rmsnorm(field, gain_row):
     return field * lax.rsqrt(jnp.mean(field * field, -1, keepdims=True) + EPS) * gain_row
 
 
-def rotate(field, cos_table, sin_table):
-    half = field.shape[-1] // 2
-    first, second = field[..., :half], field[..., half:]
-    return jnp.concatenate(
-        [first * cos_table - second * sin_table, second * cos_table + first * sin_table], -1
-    )
-
-
 def rotary_tables(length):
-    position = jnp.arange(length).astype(F32)
-    freq = THETA ** (-(jnp.arange(HD // 2).astype(F32) * 2.0 / HD))
-    angle = position[:, None] * freq[None, :]
-    return jnp.cos(angle), jnp.sin(angle)
+    freq = (THETA ** (-(np.arange(HD // 2) * 2.0 / HD))).astype(np.float32)
+    angle = (np.arange(length, dtype=np.float32)[:, None] * freq[None, :]).astype(np.float64)
+    cos, sin = np.cos(angle).astype(np.float32), np.sin(angle).astype(np.float32)
+    return np.concatenate([cos, cos], 1), np.concatenate([-sin, sin], 1)
 
 
 def dot(a, b, ca, cb):
@@ -615,8 +816,9 @@
     normed_all, meta_all, w_head = front(normed, meta, qkv_weight)
     projected = dot(normed_all, w_head, 1, 1)
     cos_table, sin_table = rotary_tables(seq)
-    q = rotate(projected[:, :HD], cos_table, sin_table).astype(BF)
-    k = rotate(projected[:, HD : 2 * HD], cos_table, sin_table).astype(BF)
+    turn = lambda a: a * cos_table + jnp.roll(a, HD // 2, 1) * sin_table
+    q = turn(projected[:, :HD]).astype(BF)
+    k = turn(projected[:, HD : 2 * HD]).astype(BF)
     v = projected[:, 2 * HD :].astype(BF)
     sq = segments[:, None]
     sk = jnp.where(segments == 0, -1, segments)[None, :]
@@ -640,10 +842,7 @@
     )
     flat = lambda a: a.reshape(-1, a.shape[2])
     xr, pg, hidden, gg, ug = [flat(a) for a in (xr, pg, hidden, gg, ug)]
-    down_g = dot(hidden, pg, 0, 0)
-    gate_g = dot(xr, gg, 0, 0)
-    up_g = dot(xr, ug, 0, 0)
-    mixture = scatter(mix_part.reshape(seq, width), 5)
+    mixture, gate_g, up_g, down_g = expert_weights(mix_part, xr, pg, hidden, gg, ug, 5)
     layer = middle + mixture
     own_seg = lax.dynamic_slice_in_dim(segments, me * rows, rows)
     valid = (own_seg != 0).astype(F32)
@@ -660,30 +859,24 @@
     middle_grad = grad + mg
     attended_grad = middle_grad.astype(BF)
     context_grad = dot(attended_grad, dense_out, 1, 0).astype(BF)
-    cg_h = swap(context_grad.reshape(rows, H, HD).transpose(1, 0, 2), 7).reshape(seq, HD)
-    dq, dkt, dvt = attend_back(q, k, v, sq, sk, lse, cg_h)
-    pgrad = jnp.concatenate(
-        [rotate(dq, cos_table, -sin_table), rotate(dkt.T, cos_table, -sin_table), dvt.T], 1
-    ).astype(BF)
-    qkv_part = dot(pgrad, normed_all, 0, 0)
-    qkv_sum = lax.psum(qkv_part.astype(BF), "grp")
-    qkv_total = give_back(qkv_sum.reshape(3, HD, width), 8).reshape(3 * HD, width).astype(F32)
-    normed_grad = scatter(dot(pgrad, w_head, 1, 0).astype(BF), 9)
-    out_part = scatter(dot(attended_grad, context, 0, 0).astype(BF), 10)
+    normed_grad, out_total, qkv_total = back(
+        context_grad, q, k, v, sq, sk, lse, cos_table, sin_table, w_head, normed_all, attended_grad, context, 6
+    )
     sg, gain1 = jax.vjp(rmsnorm, stream, norm_gain[0])[1](normed_grad)
     tokens_grad = middle_grad + sg
     seq_sums, gain_dp = lax.psum((sums, jnp.stack([gain1, gain2])), "dp")
     stat_row = jnp.sqrt(seq_sums[:3] / seq_sums[3]).reshape(1, 3)
-    over = lambda a: lax.psum(a.astype(BF), "grp").astype(F32)
+    groups = lax.axis_size("grp")
+    over = lambda a: a.astype(F32) if groups == 2 else lax.psum(a.astype(BF), "grp").astype(F32) * 0.5
     return (
         layer.astype(BF),
         tokens_grad,
-        qkv_total,
-        over(out_part),
+        over(qkv_total),
+        over(out_total),
         over(gate_g)[None],
         over(up_g)[None],
         over(down_g)[None],
-        over(gain_dp),
+        lax.psum(gain_dp.astype(BF), "grp").astype(F32),
         stat_row,
     )
 

time: 1110 us -> 942 us (0.85)
  Pallas kernels: 872 us -> 777 us
  matrix products: 66.1 us -> 19.5 us
  other arithmetic: 53.7 us -> 29.5 us
  between operations: 16.1 us -> 2.39 us
    pallas_call x5 -> x2, Pallas kernels: 306 us -> 244 us  [the longest x1 159 us: back(): pl.pallas_call(back_kernel, out_shape=[jax.ShapeDtypeStruct((rows, width)...]
    dot_general x9 -> x3, matrix products: 66.1 us -> 19.5 us  [dot(): lax.dot_general(a, b, (((ca,), (cb,)), ((), ())), preferred_element_type=...]
    pallas_call x2 -> x1, Pallas kernels: 33 us -> 9.75 us  [swap(): pl.pallas_call(swap_kernel, out_shape=jax.ShapeDtypeStruct(x.shape, x.dty...]
    unnamed x66 -> x37, local copies, waits for them, and re-layouts: 6.3 us -> 21 us
    broadcast_in_dim x3 -> x0, other arithmetic: 13.3 us -> none  [the longest x1 4.45 us: per_device(): over(down_g)[None]]
  transfers between devices with their start and end apart: 1 -> 0, of which waited for: 0 -> 0; matrix products, arithmetic and copies ran while one was open for 2% -> 0% of each run, Pallas kernels for 9% -> 0%
where the time goes in v3:
time: 942 us; the launch traced here: 934 us
  Pallas kernels  777 us (82%)
  blocking collectives  77.7 us (8%)
  other arithmetic  29.5 us (3%)
  local copies, waits for them, and re-layouts  27.3 us (3%)
  matrix products  19.5 us (2%)
    pallas_call x1, Pallas kernels, expert(): pl.pallas_call(expert_kernel, out_shape=[jax.ShapeDtypeStruct((rows, widt...  301 us
    pallas_call x1, Pallas kernels, back(): pl.pallas_call(back_kernel, out_shape=[jax.ShapeDtypeStruct((rows, width)...  159 us
    pallas_call x1, Pallas kernels, front(): pl.pallas_call(front_kernel, out_shape=[jax.ShapeDtypeStruct((16 * rows,...  125 us
    pallas_call x1, Pallas kernels, gather(): pl.pallas_call(gather_kernel, out_shape=jax.ShapeDtypeStruct((16 * rows,...  86 us
    pallas_call x1, Pallas kernels, expert_weights(): pl.pallas_call(weights_kernel, out_shape=[jax.ShapeDtypeStruct((rows, wid...  85.9 us
    psum x1, blocking collectives, per_device(): seq_sums, gain_dp = lax.psum((sums, jnp.stack([gain1, gain2])), 'dp')  61.2 us
    unnamed x37, local copies, waits for them, and re-layouts  21 us
    dot_general x3, matrix products, dot(): lax.dot_general(a, b, (((ca,), (cb,)), ((), ())), preferred_element_type=...  19.5 us

profile of v3, /device:TPU:5, one launch (start us, length us, event | category | flops | bytes accessed | tf_op | source)
XLA Modules:
  0.0 933.7 jit_solution(7828541053944840422)
XLA Ops:
  1.3 1.2 fusion.6
  2.5 0.7 convert_bitcast_fusion
  3.2 1.3 pad_maximum_fusion.1.m_ref
  4.5 0.7 compare_select_fusion
  5.2 0.8 fusion.22
  6.0 2.0 fusion.2.n_ref
  8.0 1.1 copy.39.sq
  9.1 0.0 copy-start
  9.1 86.0 %gather_2.1 = bf16[2048,2048]{1,0:T(8,128)(2,1)} custom-call(bf16[128,2048]{1,0:T(8,128)(2,1)} %x_ref.1), custom_call_target="tpu_custom_call" | custom-call | tf_op jit(solution)/shard_map/gather_2/pallas_call | solution.py:294
  95.1 125.0 %front.1 = (bf16[2048,2048]{1,0:T(8,128)(2,1)}, f32[16,16,128]{2,1,0:T(8,128)}, bf16[384,2048]{1,0:T(8,128)(2,1)}) custom-call(bf16[128,2048]{1,0:T(8,128)(2,1)} %fusion.2.n_ref, f32[16,128]{1,0:T(8,128)} %pad_maximum_fusion.1.m_ref, bf16[384,2048]{1,0:T(8,128)(2,1)} %w_ref.1), custom_call_target="tpu_custom_call" | custom-call | tf_op jit(solution)/shard_map/front/pallas_call | solution.py:267
  220.2 1.1 select_reduce_fusion.1
  221.2 0.1 copy.41
  221.4 0.1 reduce.1
  221.5 0.3 reduce_window_sum.18
  221.8 0.1 fusion.16
  221.9 0.4 select_reduce_fusion
  222.2 0.8 fusion.15.pick
  223.1 1.6 fusion.13.pickt
  224.6 1.1 copy.42.sw
  225.7 7.4 fusion.23
  233.1 0.0 copy-start.9
  233.2 0.0 copy-start.10
  233.2 0.1 slice.82.v
  233.2 0.0 copy-start.3
  233.2 0.7 fusion.21
  233.9 0.6 copy-done.9
  234.6 0.3 copy-done.10
  234.9 0.7 fusion.9
  235.5 0.0 copy-start.2
  235.6 0.0 copy-start.1
  235.6 0.0 copy-done.6
  235.6 0.0 copy-done
  235.6 0.0 copy-done.3
  235.6 10.6 %attend.1 = (bf16[2048,128]{1,0:T(8,128)(2,1)S(1)}, f32[2048,1]{1,0:T(8,128)S(1)}) custom-call(bf16[2048,128]{1,0:T(8,128)(2,1)S(1)} %get-tuple-element.69.q, bf16[2048,128]{1,0:T(8,128)(2,1)S(1)} %get-tuple-element.68.k, bf16[2048,128]{1,0:T(8,128)(2,1)S(1)} %slice.82.v, s32[2048,1]{1,0:T(8,128)S(1)} %copy.39.sq, s32[1,2048]{1,0:T(1,128)S(1)} %bitcast.49), custom_call_target="tpu_custom_call" | custom-call | tf_op jit(solution)/shard_map/attend/pallas_call | solution.py:349
  246.2 0.0 copy-start.4
  246.2 1.0 copy-done.4
  247.2 0.8 copy-done.5
  248.0 9.8 %swap_1.1 = bf16[16,128,128]{2,1,0:T(8,128)(2,1)} custom-call(bf16[16,128,128]{2,1,0:T(8,128)(2,1)} %bitcast.48), custom_call_target="tpu_custom_call" | custom-call | tf_op jit(solution)/shard_map/swap_1/pallas_call | solution.py:320
  257.7 1.9 copy_bitcast_fusion.ctx
  259.7 6.6 multiply_reduce_fusion.5
  266.3 0.9 multiply_convert_fusion.n2
  267.3 301.4 %expert.1 = (f32[128,2048]{1,0:T(8,128)}, bf16[16,128,2048]{2,1,0:T(8,128)(2,1)}, bf16[4,320,2048]{2,1,0:T(8,128)(2,1)}, bf16[4,320,2048]{2,1,0:T(8,128)(2,1)}, ...) custom-call(bf16[128,2048]{1,0:T(8,128)(2,1)} %multiply_convert_fusion.n2, ...), custom_call_target="tpu_custom_call" | custom-call | tf_op jit(solution)/shard_map/expert/pallas_call | solution.py:468
  568.7 85.9 %expert_weights.1 = (f32[128,2048]{1,0:T(8,128)}, f32[2048,1024]{1,0:T(8,128)}, f32[2048,1024]{1,0:T(8,128)}, f32[1024,2048]{1,0:T(8,128)}) custom-call(bf16[16,128,2048]{2,1,0:T(8,128)(2,1)} %get-tuple-element.32.p1, bf16[1280,2048]{1,0:T(8,128)(2,1)} %bitcast.58, bf16[1280,2048]{1,0:T(8,128)(2,1)} %bitcast.59, bf16[1280,1024]{1,0:T(8,128)(2,1)} %bitcast.63, ...), custom_call_target="tpu_custom_call" | custom-call | tf_op jit(solution)/shard_map/expert_weights/pallas_call | solution.py:586
  654.6 2.5 multiply_reduce_fusion.2
  657.1 1.4 select_reduce_fusion.4
  659.1 2.0 pad_maximum_fusion.2
  661.2 1.7 fusion.20.ag
  662.9 0.0 copy-start.8
  662.9 0.8 copy-done.8
  663.7 5.5 convolution_convert_fusion.cg
  669.1 158.6 %back.1 = (f32[128,2048]{1,0:T(8,128)}, bf16[128,2048]{1,0:T(8,128)(2,1)}, bf16[384,2048]{1,0:T(8,128)(2,1)}) custom-call(bf16[128,2048]{1,0:T(8,128)(2,1)} %convolution_convert_fusion.cg, bf16[2048,128]{1,0:T(8,128)(2,1)} %copy-done.2, bf16[2048,128]{1,0:T(8,128)(2,1)} %copy-done.1, bf16[2048,128]{1,0:T(8,128)(2,1)} %copy-done.3, s32[2048,1]{1,0:T(8,128)} %copy-done, ...), custom_call_target="tpu_custom_call" | custom-call | tf_op jit(solution)/shard_map/back/pallas_call | solution.py:766
  827.7 1.7 fusion.3
  829.5 61.2 %all-reduce = (bf16[2,2048]{1,0:T(2,128)(2,1)S(1)}, f32[4]{0:T(128)S(1)}) all-reduce(f32[2,2048]{1,0:T(2,128)S(1)} %pad_maximum_fusion, f32[4]{0:T(128)S(1)} %pad_maximum_fusion.2), channel_id=1, replica_groups=mesh['grp'=2,'dp'=16] {'dp'}, use_global_device_ids=true, to_apply=%region_12.13 | all-reduce | flops 4100 | bytes 24608 | tf_op jit(solution)/shard_map/psum | solution.py:867
  890.7 0.6 slice.60
  891.3 16.5 %psum.22 = bf16[2,2048]{1,0:T(2,128)(2,1)S(1)} all-reduce(bf16[2,2048]{1,0:T(2,128)(2,1)S(1)} %get-tuple-element.62), channel_id=1, replica_groups=mesh['grp'=2,'dp'=16] {'grp'}, use_global_device_ids=true, to_apply=%region_13.14 | all-reduce | flops 4096 | bytes 16384 | tf_op jit(solution)/shard_map/psum | solution.py:879
  907.8 1.3 sqrt_bitcast_fusion
  909.1 3.2 fusion.5
  912.3 0.6 convert_element_type.82
  912.9 1.1 convert_element_type.80
  914.0 2.0 convert_element_type.79
  916.0 8.8 copy.54
  924.9 4.3 copy.55
  929.1 1.0 slice-done.1
  930.1 3.4 copy.56
  (25 shorter events, 0.1 us)
Async XLA Ops:
  5.2 230.4 %copy-start.6 = (s32[2048]{0:T(1024)}, s32[2048]{0:T(1024)S(1)}, u32[]{:S(2)}) copy-start(s32[2048]{0:T(1024)S(1)} %compare_select_fusion) | copy-start | bytes 24580
  9.1 226.5 %copy-start = (s32[2048,1]{1,0:T(8,128)}, s32[2048,1]{1,0:T(8,128)S(1)}, u32[]{:S(2)}) copy-start(s32[2048,1]{1,0:T(8,128)S(1)} %copy.39.sq) | copy-start | bytes 24580
  233.1 1.4 copy-start.9
  233.2 1.7 copy-start.10
  233.2 2.4 copy-start.3
  234.9 24.8 %copy-start.7 = (bf16[128,2048]{1,0:T(8,128)(2,1)S(1)}, bf16[128,2048]{1,0:T(8,128)(2,1)}, u32[]{:S(2)}) copy-start(bf16[128,2048]{1,0:T(8,128)(2,1)} %param.14) | copy-start | bytes 1572868
  235.5 10.7 %copy-start.2 = (bf16[2048,128]{1,0:T(8,128)(2,1)}, bf16[2048,128]{1,0:T(8,128)(2,1)S(1)}, u32[]{:S(2)}) copy-start(bf16[2048,128]{1,0:T(8,128)(2,1)S(1)} %get-tuple-element.69.q) | copy-start | bytes 1572868
  235.6 30.7 %copy-start.1 = (bf16[2048,128]{1,0:T(8,128)(2,1)}, bf16[2048,128]{1,0:T(8,128)(2,1)S(1)}, u32[]{:S(2)}) copy-start(bf16[2048,128]{1,0:T(8,128)(2,1)S(1)} %get-tuple-element.68.k) | copy-start | bytes 1572868
  246.2 1.0 copy-start.4
  247.2 0.8 copy-start.5
  662.9 0.8 copy-start.8
  827.7 85.2 %copy-start.12 = (bf16[128,2048]{1,0:T(8,128)(2,1)S(1)}, bf16[128,2048]{1,0:T(8,128)(2,1)}, u32[]{:S(2)}) copy-start(bf16[128,2048]{1,0:T(8,128)(2,1)} %get-tuple-element.43) | copy-start | bytes 1572868
  907.8 6.2 copy-start.11
  914.0 10.8 %slice-start.2 = ((s8[8388608]{0:T(1024)(128)(4,1)}), s8[4194304]{0:T(1024)(128)(4,1)S(1)}, s32[]{:S(2)}) async-start(s8[8388608]{0:T(1024)(128)(4,1)} %bitcast.54), calls=%async_computation.2 | async-start | bytes 8388608
  916.0 8.8 slice-start.3
  916.0 13.1 %slice-start = ((s8[8388608]{0:T(1024)(128)(4,1)}), s8[4194304]{0:T(1024)(128)(4,1)S(1)}, s32[]{:S(2)}) async-start(s8[8388608]{0:T(1024)(128)(4,1)} %bitcast.51), calls=%async_computation | async-start | bytes 8388608
  924.9 5.2 slice-start.1

commit v4 on v3

--- a/solution.py
+++ b/solution.py
@@ -73,15 +73,15 @@
 
 
 class Gather:
-    def __init__(self, src, dst, rows, sems):
-        self.src, self.dst, self.rows, self.sems, self.p = src, dst, rows, sems, places()
+    def __init__(self, src, dst, rows, sems, first=0):
+        self.src, self.dst, self.rows, self.sems, self.first, self.p = src, dst, rows, sems, first, places()
 
     def block(self, b):
-        return self.dst.at[pl.ds(pl.multiple_of(b * self.rows, self.rows), self.rows)]
+        return self.dst.at[b, pl.ds(self.first, self.rows)]
 
     def part(self, b, h):
         half = self.rows // 2
-        return self.dst.at[pl.ds(pl.multiple_of(b * self.rows + h * half, half), half)]
+        return self.dst.at[b, pl.ds(self.first + h * half, half)]
 
     def begin(self):
         zs, zr, xs, xr, ys, yr, _, _, own = self.sems
@@ -210,26 +210,27 @@
     return pltpu.CompilerParams(collective_id=cid, has_side_effects=True, vmem_limit_bytes=vmem * MIB)
 
 
-def front_kernel(n_ref, m_ref, w_ref, nall, mall, wh, *sems):
-    g_sems, (ms, mr, mo, ws, wr, ps, pr, wo) = sems[:9], sems[9:]
+def front_kernel(
+    n_ref, m_ref, w_ref, o_ref, cosf, sinf, sq, sk,
+    nall_o, mall, wh_o, q, k, v, lse, ctx, oall,
+    nall, wh, ctxh, ms, mr, mo, ws, wr, ps, pr, wo, no, cs, cr, co, os_, or_, *sems,
+):
     me = lax.axis_index("dp")
     core = lax.axis_index("grp") % 2
+    hr = HD // 2
+    blk = lambda b: pl.ds(pl.multiple_of(b * HD, HD), HD)
+    half = lambda s, c: pl.ds(pl.multiple_of(s * HD + c * hr, hr), hr)
     barrier([lax.rem(me + d, 16) for d in range(1, 16)], pair=True)
-    hr = HD // 2
-    g = Gather(n_ref, nall, n_ref.shape[0], g_sems)
+    g = Gather(n_ref, nall, n_ref.shape[0], sems[:9])
+    go = Gather(o_ref.at[half(0, core)], oall, hr, sems[9:], pl.multiple_of(core * hr, hr))
     g.begin()
     own = pltpu.make_async_copy(m_ref, mall.at[me], mo)
     own.start()
-    mc = []
-    for d in range(1, 16):
-        to = lax.rem(me + d, 16)
-        mc.append(push(m_ref, mall.at[me], ms.at[d], mr.at[d], to))
-    off = core * hr
+    mc = [push(m_ref, mall.at[me], ms.at[d], mr.at[d], lax.rem(me + d, 16)) for d in range(1, 16)]
     for l in range(3):
         b = 3 * me + l
         to, slot = lax.rem(b, 16), b // 16
-        src = w_ref.at[pl.ds(pl.multiple_of(l * HD + off, hr), hr)]
-        dst = wh.at[pl.ds(pl.multiple_of(slot * HD + off, hr), hr)]
+        src, dst = w_ref.at[half(l, core)], wh.at[half(slot, core)]
 
         @pl.when(to != me)
         def _():
@@ -239,122 +240,114 @@
         def _():
             pltpu.make_async_copy(src, dst, wr.at[slot]).start()
 
-    for s in range(3):
-        dst = wh.at[pl.ds(pl.multiple_of(s * HD + off, hr), hr)]
-        pltpu.make_async_copy(dst, dst, wr.at[s]).wait()
-        push_pair(dst, dst, ps.at[s], pr.at[s])
-    g.all()
+    for c in range(4):
+        g.step(c)
+        if c == 0:
+            pc = []
+            for s in range(3):
+                dst = wh.at[half(s, core)]
+                pltpu.make_async_copy(dst, dst, wr.at[s]).wait()
+                pc.append(push_pair(dst, dst, ps.at[s], pr.at[s]))
+            for p in pc:
+                p.wait_recv()
+        if c == 2:
+            go.begin()
+        g.ready(c)
+
+        def project(j, carry):
+            b = place_of(c, j)
+            row = blk(b)
+            out = dot(nall[b], wh[...], 1, 1)
+            turn = lambda a: (a * cosf[row] + pltpu.roll(a, HD // 2, 1) * sinf[row]).astype(BF)
+            q[row] = turn(out[:, :HD])
+            k[row] = turn(out[:, HD : 2 * HD])
+            v[row] = out[:, 2 * HD :].astype(BF)
+            return carry
+
+        lax.fori_loop(0, 4, project, 0)
+    saves = [pltpu.make_async_copy(nall, nall_o, no), pltpu.make_async_copy(wh, wh_o, wo)]
+    for c in saves:
+        c.start()
+
+    def hop(d):
+        to = lax.rem(me + d, 16)
+        return pltpu.make_async_remote_copy(
+            src_ref=ctxh.at[blk(to)], dst_ref=ctx.at[:, blk(me)], send_sem=cs.at[d], recv_sem=cr.at[d],
+            device_id={"dp": to}, device_id_type=MESH,
+        )
+
+    def attend_rows(d, carry):
+        row = blk(lax.rem(me + d, 16))
+        s = dot(q[row], k[...], 1, 1)
+        s = jnp.where(sq[row] == sk[...], s, -1e30)
+        peak = jnp.maximum(jnp.max(s, -1, keepdims=True), -1e29)
+        ex = jnp.exp2((s - peak) * (SCALE * LOG2E))
+        total = jnp.maximum(jnp.sum(ex, -1, keepdims=True), 1.0)
+        prob = (ex * (1.0 / total)).astype(BF)
+        ctxh[row] = jnp.dot(prob, v[...], preferred_element_type=F32).astype(BF)
+        lse[row] = peak * (SCALE * LOG2E) + jnp.log2(total)
+        return carry
+
+    def attend_send(d, carry):
+        attend_rows(d, carry)
+        hop(d).start()
+        return carry
+
+    lax.fori_loop(1, 8, attend_send, 0)
+    go.step(0)
+    lax.fori_loop(8, 16, attend_send, 0)
+    attend_rows(0, 0)
+    stay = pltpu.make_async_copy(ctxh.at[blk(me)], ctx.at[:, blk(me)], co)
+    stay.start()
+    for c in (1, 2, 3):
+        go.step(c)
+    for c in range(4):
+        go.ready(c)
+    here = oall.at[:, pl.ds(pl.multiple_of(core * hr, hr), hr)]
+    oc = push_pair(here, here, os_, or_)
+    g.end()
+    go.end()
     own.wait()
     for c in mc:
         c.wait()
     for l in range(3):
-        b = 3 * me + l
-        src = w_ref.at[pl.ds(pl.multiple_of(l * HD + off, hr), hr)]
-
-        @pl.when(lax.rem(b, 16) != me)
+        src = w_ref.at[half(l, core)]
+
+        @pl.when(lax.rem(3 * me + l, 16) != me)
         def _():
             pltpu.make_async_copy(src, src, ws.at[l]).wait()
 
-    for s in range(3):
-        dst = wh.at[pl.ds(pl.multiple_of(s * HD + off, hr), hr)]
-        other = wh.at[pl.ds(pl.multiple_of(s * HD + (hr - off), hr), hr)]
-        pltpu.make_async_copy(dst, dst, ps.at[s]).wait()
-        pltpu.make_async_copy(other, other, pr.at[s]).wait()
-
-
-def front(normed, meta, w):
+    for p in pc:
+        p.wait_send()
+    for c in saves:
+        c.wait()
+    stay.wait()
+    for d in range(1, 16):
+        hop(d).wait()
+    oc.wait()
+
+
+def front(normed, meta, w, wo, cosf, sinf, sq, sk, cid):
     rows, width = normed.shape
+    seq = cosf.shape[0]
+    sem = lambda *shape: pltpu.SemaphoreType.DMA(shape) if shape else pltpu.SemaphoreType.DMA
+    b = lambda *shape: jax.ShapeDtypeStruct(shape, BF)
+    f = lambda *shape: jax.ShapeDtypeStruct(shape, F32)
     return pl.pallas_call(
         front_kernel,
         out_shape=[
-            jax.ShapeDtypeStruct((16 * rows, width), BF),
-            jax.ShapeDtypeStruct((16,) + meta.shape, F32),
-            jax.ShapeDtypeStruct((3 * HD, width), BF),
+            b(16, rows, width), f(16, *meta.shape), b(3 * HD, width),
+            b(seq, HD), b(seq, HD), b(seq, HD), f(seq, 1), b(rows, width), b(16, rows, width),
         ],
-        in_specs=[ANY] * 3,
-        out_specs=[ANY] * 3,
-        scratch_shapes=GATHER_SEMS
-        + [pltpu.SemaphoreType.DMA((16,)), pltpu.SemaphoreType.DMA((16,)), pltpu.SemaphoreType.DMA]
-        + [pltpu.SemaphoreType.DMA((3,))] * 4
-        + [pltpu.SemaphoreType.DMA],
-        compiler_params=params(0),
+        in_specs=[ANY] * 4 + [VM] * 4,
+        out_specs=[ANY] * 3 + [VM] * 4 + [ANY] * 2,
+        scratch_shapes=[pltpu.VMEM((16, rows, width), BF), pltpu.VMEM((3 * HD, width), BF), pltpu.VMEM((seq, HD), BF)]
+        + [sem(16), sem(16), sem(), sem(3), sem(3), sem(3), sem(3), sem(), sem()]
+        + [sem(16), sem(16), sem(), sem(), sem()]
+        + GATHER_SEMS * 2,
+        compiler_params=params(cid),
         name="front",
-    )(normed, meta, w)
-
-
-def gather_kernel(x_ref, o_ref, *sems):
-    barrier(gather_targets())
-    g = Gather(x_ref, o_ref, x_ref.shape[0], sems)
-    g.begin()
-    g.all()
-
-
-def gather(x, cid):
-    rows, width = x.shape
-    return pl.pallas_call(
-        gather_kernel,
-        out_shape=jax.ShapeDtypeStruct((16 * rows, width), x.dtype),
-        in_specs=[ANY],
-        out_specs=ANY,
-        scratch_shapes=GATHER_SEMS,
-        compiler_params=params(cid),
-        name=f"gather_{cid}",
-    )(x)
-
-
-def swap_kernel(x_ref, o_ref, ss, rs, lo):
-    me = lax.axis_index("dp")
-    barrier([lax.rem(me + d, 16) for d in range(1, 16)])
-    own = pltpu.make_async_copy(x_ref.at[me], o_ref.at[me], lo)
-    own.start()
-    sent = []
-    for d in range(1, 16):
-        to = lax.rem(me + d, 16)
-        sent.append(push(x_ref.at[to], o_ref.at[me], ss.at[d], rs.at[d], to))
-    own.wait()
-    for c in sent:
-        c.wait()
-
-
-def swap(x, cid):
-    return pl.pallas_call(
-        swap_kernel,
-        out_shape=jax.ShapeDtypeStruct(x.shape, x.dtype),
-        in_specs=[ANY],
-        out_specs=ANY,
-        scratch_shapes=[pltpu.SemaphoreType.DMA((16,))] * 2 + [pltpu.SemaphoreType.DMA],
-        compiler_params=params(cid),
-        name=f"swap_{cid}",
-    )(x)
-
-
-QB = 256
-
-
-def attend_kernel(q, k, v, sq, sk, ctx, lse):
-    s = lax.dot_general(q[...], k[...], (((1,), (1,)), ((), ())), preferred_element_type=F32)
-    s = jnp.where(sq[...] == sk[...], s, -1e30)
-    peak = jnp.maximum(jnp.max(s, -1, keepdims=True), -1e29)
-    ex = jnp.exp2((s - peak) * (SCALE * LOG2E))
-    total = jnp.maximum(jnp.sum(ex, -1, keepdims=True), 1.0)
-    prob = (ex * (1.0 / total)).astype(BF)
-    ctx[...] = jnp.dot(prob, v[...], preferred_element_type=F32).astype(BF)
-    lse[...] = peak * (SCALE * LOG2E) + jnp.log2(total)
-
-
-def attend(q, k, v, sq, sk):
-    n = q.shape[0]
-    row = lambda w: pl.BlockSpec((QB, w), lambda i: (i, 0))
-    full = lambda r, w: pl.BlockSpec((r, w), lambda i: (0, 0))
-    return pl.pallas_call(
-        attend_kernel,
-        grid=(n // QB,),
-        out_shape=[jax.ShapeDtypeStruct((n, HD), BF), jax.ShapeDtypeStruct((n, 1), F32)],
-        in_specs=[row(HD), full(n, HD), full(n, HD), row(1), full(1, n)],
-        out_specs=[row(HD), row(1)],
-        compiler_params=pltpu.CompilerParams(vmem_limit_bytes=48 * MIB),
-        name="attend",
-    )(q, k, v, sq, sk)
+    )(normed, meta, w, wo, cosf, sinf, sq, sk)
 
 
 SLOTS = 80
@@ -399,16 +392,15 @@
 
         def collect(j, carry):
             b = place_of(k, j)
-            row = pl.ds(pl.multiple_of(b * rows, rows), rows)
             to = pl.ds(pl.multiple_of(j * SLOTS, SLOTS), SLOTS)
 
             def cols(n, c):
                 w = pl.ds(pl.multiple_of(n * 512, 512), 512)
-                xr[to, w] = dot(pick[b], nall[row, w], 1, 0).astype(BF)
-                pg[to, w] = (dot(pick[b], call[row, w], 1, 0) * sw[b]).astype(BF)
+                xr[to, w] = dot(pick[b], nall[b, :, w], 1, 0).astype(BF)
+                pg[to, w] = (dot(pick[b], call[b, :, w], 1, 0) * sw[b]).astype(BF)
                 return c
 
-            return lax.fori_loop(0, nall.shape[1] // 512, cols, carry)
+            return lax.fori_loop(0, nall.shape[2] // 512, cols, carry)
 
         lax.fori_loop(0, 4, collect, 0)
 
@@ -475,7 +467,7 @@
         in_specs=[ANY, ANY, VM, VM, VM, ANY, ANY, ANY],
         out_specs=[VM] + [ANY] * 6,
         scratch_shapes=[
-            v(16 * rows, width), v(16 * rows, width), v(16, rows, width), v(4, rows, width),
+            v(16, rows, width), v(16, rows, width), v(16, rows, width), v(4, rows, width),
             v(width, ff), v(width, ff), v(ff, width),
             v(chunk, width), v(chunk, width), v(chunk, ff), v(chunk, ff), v(chunk, ff),
         ]
@@ -540,7 +532,7 @@
         def finish(t, m=m):
             s = lax.rem(t, 2)
             sent(t, m).wait_recv()
-            own[s] = own[s] + got[m, t].astype(F32)
+            own[s] = (own[s].astype(F32) + got[m, t].astype(F32)).astype(BF)
             saved(t, m).start()
 
         def body(t, carry, m=m):
@@ -553,7 +545,7 @@
 
             low = product(m, t).astype(BF)
             give[s] = low
-            own[s] = low.astype(F32)
+            own[s] = low
             sent(t, m).start()
 
             @pl.when(t >= 1)
@@ -587,15 +579,15 @@
         weights_kernel,
         out_shape=[
             jax.ShapeDtypeStruct((rows, width), F32),
-            jax.ShapeDtypeStruct((width, ff), F32),
-            jax.ShapeDtypeStruct((width, ff), F32),
-            jax.ShapeDtypeStruct((ff, width), F32),
+            jax.ShapeDtypeStruct((width, ff), BF),
+            jax.ShapeDtypeStruct((width, ff), BF),
+            jax.ShapeDtypeStruct((ff, width), BF),
         ],
         in_specs=[ANY] * 6,
         out_specs=[VM] + [ANY] * 3,
         scratch_shapes=[
             v(16, rows, width), v(n, width), v(n, width), v(n, ff), v(n, ff), v(n, ff),
-            pltpu.VMEM((2, r, w), F32), v(2, r, w), v(3, 8, r, w),
+            v(2, r, w), v(2, r, w), v(3, 8, r, w),
         ]
         + scatter_bufs(rows, width)
         + [pltpu.SemaphoreType.DMA, pltpu.SemaphoreType.DMA((6,)), pltpu.SemaphoreType.DMA((2,))]
@@ -787,6 +779,37 @@
     )(cg, q, k, v, sq, sk, lse, cosf, sinf, wh, nall, ag, ctx)
 
 
+def total_kernel(x, dp_o, pair_o, got, fromp, ss, rs, ps, pr):
+    me = lax.axis_index("dp")
+    barrier([lax.rem(me + d, 16) for d in range(1, 16)], pair=True)
+    sent = [push(x, got.at[me], ss.at[d], rs.at[d], lax.rem(me + d, 16)) for d in range(1, 16)]
+    got[me] = x[...]
+    for c in sent:
+        c.wait_recv()
+    acc = got[0]
+    for j in range(1, 16):
+        acc = acc + got[j]
+    dp_o[...] = acc
+    c = push_pair(dp_o, fromp, ps, pr)
+    c.wait()
+    pair_o[...] = acc + fromp[...]
+    for c in sent:
+        c.wait_send()
+
+
+def total(x, cid):
+    sem = pltpu.SemaphoreType.DMA
+    return pl.pallas_call(
+        total_kernel,
+        out_shape=[jax.ShapeDtypeStruct(x.shape, F32)] * 2,
+        in_specs=[VM],
+        out_specs=[VM, VM],
+        scratch_shapes=[pltpu.VMEM((16,) + x.shape, F32), pltpu.VMEM(x.shape, F32), sem((16,)), sem((16,)), sem, sem],
+        compiler_params=params(cid, 16),
+        name="total",
+    )(x)
+
+
 def rmsnorm(field, gain_row):
     return field * lax.rsqrt(jnp.mean(field * field, -1, keepdims=True) + EPS) * gain_row
 
@@ -813,18 +836,14 @@
     stream = tokens.astype(F32)
     normed = rmsnorm(stream, norm_gain[0]).astype(BF)
     meta = jnp.concatenate([routes.astype(F32).T, route_weight.T], 0)
-    normed_all, meta_all, w_head = front(normed, meta, qkv_weight)
-    projected = dot(normed_all, w_head, 1, 1)
-    cos_table, sin_table = rotary_tables(seq)
-    turn = lambda a: a * cos_table + jnp.roll(a, HD // 2, 1) * sin_table
-    q = turn(projected[:, :HD]).astype(BF)
-    k = turn(projected[:, HD : 2 * HD]).astype(BF)
-    v = projected[:, 2 * HD :].astype(BF)
     sq = segments[:, None]
     sk = jnp.where(segments == 0, -1, segments)[None, :]
-    ctx_h, lse = attend(q, k, v, sq, sk)
-    context = swap(ctx_h.reshape(16, rows, HD), 1).transpose(1, 0, 2).reshape(rows, width)
-    dense_out = gather(out_weight, 2)
+    cos_table, sin_table = rotary_tables(seq)
+    normed_all, meta_all, w_head, q, k, v, lse, context, dense_out = front(
+        normed, meta, qkv_weight, out_weight, cos_table, sin_table, sq, sk, 0
+    )
+    normed_all = normed_all.reshape(seq, width)
+    dense_out = dense_out.reshape(seq, width)
     attended = dot(context, dense_out, 1, 1)
     middle = stream + attended
     normed2 = rmsnorm(middle, norm_gain[1]).astype(BF)
@@ -864,7 +883,10 @@
     )
     sg, gain1 = jax.vjp(rmsnorm, stream, norm_gain[0])[1](normed_grad)
     tokens_grad = middle_grad + sg
-    seq_sums, gain_dp = lax.psum((sums, jnp.stack([gain1, gain2])), "dp")
+    small = jnp.concatenate([gain1, gain2, sums, jnp.zeros((1024 - sums.size,), F32)]).reshape(-1, HD)
+    in_group, in_pair = total(small, 4)
+    seq_sums = in_group.reshape(-1)[2 * width : 2 * width + 4]
+    gain_pair = in_pair.reshape(-1)[: 2 * width].reshape(2, width)
     stat_row = jnp.sqrt(seq_sums[:3] / seq_sums[3]).reshape(1, 3)
     groups = lax.axis_size("grp")
     over = lambda a: a.astype(F32) if groups == 2 else lax.psum(a.astype(BF), "grp").astype(F32) * 0.5
@@ -876,7 +898,7 @@
         over(gate_g)[None],
         over(up_g)[None],
         over(down_g)[None],
-        lax.psum(gain_dp.astype(BF), "grp").astype(F32),
+        gain_pair if groups == 2 else lax.psum(gain_pair, "grp") * 0.5,
         stat_row,
     )
 

time: 942 us -> 844 us (0.90)
  blocking collectives: 77.7 us -> 0 us
  local copies, waits for them, and re-layouts: 27.3 us -> 7.36 us
  Pallas kernels: 777 us -> 765 us
  other arithmetic: 29.5 us -> 41.4 us
    psum x2 -> x0, blocking collectives: 77.7 us -> none  [the longest x1 61.2 us: per_device(): seq_sums, gain_dp = lax.psum((sums, jnp.stack([gain1, gain2])), 'dp')]
    pallas_call x4 -> x2, Pallas kernels: 231 us -> 201 us  [the longest x1 178 us: front(): pl.pallas_call(front_kernel, out_shape=[b(16, rows, width), f(16, *meta.s...]
    unnamed x37 -> x16, local copies, waits for them, and re-layouts: 21 us -> 0.07 us
    broadcast_in_dim x0 -> x2, other arithmetic: none -> 16.6 us  [the longest x1 12.1 us: per_device(): over(up_g)[None]]
    pallas_call x1, Pallas kernels: 85.9 us -> 102 us  [expert_weights(): pl.pallas_call(weights_kernel, out_shape=[jax.ShapeDtypeStruct((rows, wid...]
    dot_general x3 -> x2, matrix products: 19.5 us -> 12.2 us  [dot(): lax.dot_general(a, b, (((ca,), (cb,)), ((), ())), preferred_element_type=...]
where the time goes in v4:
time: 844 us; the launch traced here: 828 us
  Pallas kernels  765 us (91%)
  other arithmetic  41.4 us (5%)
  matrix products  12.2 us (1%)
    pallas_call x1, Pallas kernels, expert(): pl.pallas_call(expert_kernel, out_shape=[jax.ShapeDtypeStruct((rows, widt...  302 us
    pallas_call x1, Pallas kernels, front(): pl.pallas_call(front_kernel, out_shape=[b(16, rows, width), f(16, *meta.s...  178 us
    pallas_call x1, Pallas kernels, back(): pl.pallas_call(back_kernel, out_shape=[jax.ShapeDtypeStruct((rows, width)...  160 us
    pallas_call x1, Pallas kernels, expert_weights(): pl.pallas_call(weights_kernel, out_shape=[jax.ShapeDtypeStruct((rows, wid...  102 us
    pallas_call x1, Pallas kernels, total(): pl.pallas_call(total_kernel, out_shape=[jax.ShapeDtypeStruct(x.shape, F32...  23 us

profile of v4, /device:TPU:5, one launch (start us, length us, event | category | flops | bytes accessed | tf_op | source)
XLA Modules:
  0.0 828.1 jit_solution(6799709417917555895)
XLA Ops:
  0.6 0.0 copy-start
  0.7 0.8 fusion.18
  1.5 1.2 fusion.6
  2.7 2.0 fusion.2.n_ref
  4.7 2.0 copy.24.sq
  6.8 1.3 compare_select_fusion
  8.1 0.7 convert_bitcast_fusion
  8.8 1.3 pad_maximum_fusion.m_ref
  10.0 178.0 %front.1 = (bf16[16,128,2048]{2,1,0:T(8,128)(2,1)}, f32[16,16,128]{2,1,0:T(8,128)}, bf16[384,2048]{1,0:T(8,128)(2,1)}, bf16[2048,128]{1,0:T(8,128)(2,1)}, bf16[2...) custom-call(bf16[128,2048]{1,0:T(8,128)(2,1)} %fusion.2.n_ref, ...), custom_call_target="tpu_custom_call" | custom-call | tf_op jit(solution)/shard_map/front/pallas_call | solution.py:336
  188.1 1.1 select_reduce_fusion.1
  189.2 0.1 copy.25
  189.3 0.1 reduce.1
  189.4 0.3 reduce_window_sum.18
  190.3 0.1 fusion.12
  190.4 0.4 select_reduce_fusion
  190.8 1.1 copy.26.sw
  191.9 1.4 fusion.9.pickt
  193.3 0.8 fusion.11.pick
  194.2 0.0 copy-done
  194.2 6.6 multiply_reduce_fusion.5
  200.8 1.0 multiply_convert_fusion.n2
  201.7 302.2 %expert.1 = (f32[128,2048]{1,0:T(8,128)}, bf16[16,128,2048]{2,1,0:T(8,128)(2,1)}, bf16[4,320,2048]{2,1,0:T(8,128)(2,1)}, bf16[4,320,2048]{2,1,0:T(8,128)(2,1)}, ...) custom-call(bf16[128,2048]{1,0:T(8,128)(2,1)} %multiply_convert_fusion.n2, ...), custom_call_target="tpu_custom_call" | custom-call | tf_op jit(solution)/shard_map/expert/pallas_call | solution.py:460
  503.9 101.8 %expert_weights.1 = (f32[128,2048]{1,0:T(8,128)}, bf16[2048,1024]{1,0:T(8,128)(2,1)}, bf16[2048,1024]{1,0:T(8,128)(2,1)}, bf16[1024,2048]{1,0:T(8,128)(2,1)}) custom-call(bf16[16,128,2048]{2,1,0:T(8,128)(2,1)} %get-tuple-element.37.p1, bf16[1280,2048]{1,0:T(8,128)(2,1)} %bitcast.48, bf16[1280,2048]{1,0:T(8,128)(2,1)} %bitcast.49, ...), custom_call_target="tpu_custom_call" | custom-call | tf_op jit(solution)/shard_map/expert_weights/pallas_call | solution.py:578
  605.7 2.6 multiply_reduce_fusion
  608.4 1.4 convert_reduce_fusion.2
  609.7 1.7 fusion.17.ag
  611.4 0.0 copy-start.2
  611.5 5.7 convolution_convert_fusion.cg
  617.1 0.0 copy-done.2
  617.1 159.7 %back.1 = (f32[128,2048]{1,0:T(8,128)}, bf16[128,2048]{1,0:T(8,128)(2,1)}, bf16[384,2048]{1,0:T(8,128)(2,1)}) custom-call(bf16[128,2048]{1,0:T(8,128)(2,1)} %convolution_convert_fusion.cg, bf16[2048,128]{1,0:T(8,128)(2,1)} %get-tuple-element.45.q, bf16[2048,128]{1,0:T(8,128)(2,1)} %get-tuple-element.46.k, bf16[2048,128]{1,0:T(8,128)(2,1)} %get-tuple-element.47.v, ...), custom_call_target="tpu_custom_call" | custom-call | tf_op jit(solution)/shard_map/back/pallas_call | solution.py:758
  776.8 1.6 fusion.3
  779.1 2.0 concatenate.7
  781.1 23.0 %total.1 = (f32[40,128]{1,0:T(8,128)S(1)}, f32[40,128]{1,0:T(8,128)S(1)}) custom-call(f32[40,128]{1,0:T(8,128)S(1)} %bitcast.42), custom_call_target="tpu_custom_call" | custom-call | tf_op jit(solution)/shard_map/total/pallas_call | solution.py:802
  804.2 0.6 slice.35
  804.8 1.2 fusion.14
  805.9 0.6 reshape.154
  806.5 0.0 copy-start.4
  806.6 12.1 %bitcast_convert_fusion.1 = (f32[1,2048,1024]{2,1,0:T(8,128)}, f32[1,2048,1024]{2,1,0:T(8,128)}) fusion(bf16[2048,1024]{1,0:T(8,128)(2,1)} %get-tuple-element.55, bf16[2048,1024]{1,0:T(8,128)(2,1)} %get-tuple-element.54), kind=kLoop, calls=%fused_computation.1 | loop fusion | flops 4194304 | bytes 25165824 | tf_op jit(solution)/shard_map/broadcast_in_dim | solution.py:899
  818.7 0.0 copy-done.4
  818.7 0.0 copy-start.6
  818.7 0.0 copy-start.3
  818.7 4.4 bitcast_convert_fusion
  823.1 0.0 copy-start.1
  823.1 0.0 copy-start.5
  823.1 0.0 copy-start.7
  823.1 0.0 copy-done.6
  823.1 2.0 convert_element_type.67
  825.2 0.0 copy-done.3
  825.2 0.0 copy-done.1
  825.2 0.0 copy-done.5
  825.2 1.6 fusion.5
  826.8 0.0 copy-done.7
  826.8 1.1 convert_element_type.68
  (7 shorter events, 0.1 us)
Async XLA Ops:
  0.6 193.5 %copy-start = (bf16[128,2048]{1,0:T(8,128)(2,1)S(1)}, bf16[128,2048]{1,0:T(8,128)(2,1)}, u32[]{:S(2)}) copy-start(bf16[128,2048]{1,0:T(8,128)(2,1)} %param.14) | copy-start | bytes 1572868
  611.4 5.7 copy-start.2
  806.5 12.1 %copy-start.4 = (bf16[1024,2048]{1,0:T(8,128)(2,1)S(1)}, bf16[1024,2048]{1,0:T(8,128)(2,1)}, u32[]{:S(2)}) copy-start(bf16[1024,2048]{1,0:T(8,128)(2,1)} %get-tuple-element.56) | copy-start | bytes 12582916
  818.7 4.5 copy-start.6
  818.7 6.5 copy-start.3
  823.1 2.1 copy-start.1
  823.1 2.1 copy-start.5
  823.1 3.7 copy-start.7
